TPU v7x, 512 devices: a whole 4x8x8 slice. The times are simulated.
512 devices in a mesh: dp: 32 (over x_lo, z, core), seq: 16 (over x_hi, y).
Axes of the slice: x: 4 (x_hi: 2, x_lo: 2; x = x_hi * 2 + x_lo), y: 8, z: 8, core: 2. Of those that a mesh axis runs over, the one named last changes fastest.
Arguments:
- queries: bfloat16 [32, 2048, 2048], P('dp', 'seq'), may hold values from -80 to 80
- keys: bfloat16 [32, 2048, 2048], P('dp', 'seq'), may hold values from -5 to 5
- values: bfloat16 [32, 2048, 2048], P('dp', 'seq'), may hold values from -6 to 6
- grads_out: bfloat16 [32, 2048, 2048], P('dp', 'seq'), may hold values from -6 to 6
- q_scale: float32 [16, 128], replicated, may hold values from 0.5 to 2
- lengths: int32 [32], P('dp'), may hold values from 1 to 2048, 32768 in all
Outputs:
- attention_out: bfloat16 [32, 2048, 2048], P('dp', 'seq')
- query_grad: bfloat16 [32, 2048, 2048], P('dp', 'seq')
- key_grad: bfloat16 [32, 2048, 2048], P('dp', 'seq')
- value_grad: bfloat16 [32, 2048, 2048], P('dp', 'seq')
- scale_grad: float32 [16, 128], replicated
Inputs may be any that keep to these rules, and one draw needn't show every extreme that they name: `lengths`: the valid tokens of a mesh are its first ones; some mesh has all 2048 valid.
All inputs are finite; a program needn't handle non-finite values. No bound on the sum of `lengths` on one device may be relied on, other than what follows from the above.
Results may differ from a plain program's by a relative error of at most 0.007.
Values may be sent and summed in bfloat16 or wider, within the bound.
No kernel may reach another device: no remote copies, remote signals or barrier semaphores. Data moves between devices by JAX's collectives and lax.ppermute only.
A program may use at most 64 MiB of HBM per device.

v0:
```python
import math

import jax
import jax.numpy as jnp
from jax import lax
from jax.sharding import PartitionSpec as P

NEG = -1e30
BLOCK_ROWS = 512


def block_scores(scaled_rows, head_keys, key_valid, inverse):
    raw = (
        jnp.einsum("qgd,kgd->gqk", scaled_rows, head_keys, preferred_element_type=jnp.float32)
        * inverse
    )
    return jnp.where(key_valid[None, None, :], raw, NEG)


def block_output(weights_b, head_values, valid_row):
    attended = jnp.einsum(
        "gqk,kgd->qgd", weights_b, head_values, preferred_element_type=jnp.float32
    )
    return (attended * valid_row[:, None, None]).astype(jnp.bfloat16)


def block_grads(
    scaled_rows, head_keys, head_values, grad_rows, weights, weights_b, valid_row, inverse
):
    masked = grad_rows * valid_row[:, None, None].astype(jnp.bfloat16)
    dprob = jnp.einsum("qgd,kgd->gqk", masked, head_values, preferred_element_type=jnp.float32)
    delta = jnp.sum(weights * dprob, axis=2, keepdims=True)
    dscore = (weights * (dprob - delta)).astype(jnp.bfloat16)
    dvalues = jnp.einsum("gqk,qgd->kgd", weights_b, masked, preferred_element_type=jnp.float32)
    dscaled = (
        jnp.einsum("gqk,kgd->qgd", dscore, head_keys, preferred_element_type=jnp.float32) * inverse
    )
    dkeys = (
        jnp.einsum("gqk,qgd->kgd", dscore, scaled_rows, preferred_element_type=jnp.float32)
        * inverse
    )
    return (dscaled.astype(jnp.bfloat16), dkeys, dvalues)


def per_device(queries, keys, values, grads_out, q_scale, lengths):
    local_tokens = queries.shape[1]
    width = queries.shape[2]
    heads_all = q_scale.shape[0]
    head_size = q_scale.shape[1]
    groups = lax.axis_size("seq")
    mesh_len = local_tokens * groups
    local_heads = heads_all // groups
    stride = min(mesh_len, BLOCK_ROWS)
    blocks_count = mesh_len // stride
    inverse = 1.0 / math.sqrt(head_size)
    length = lengths[0]
    scale_row = q_scale.reshape(1, width)
    scaled = (queries[0].astype(jnp.float32) * scale_row).astype(jnp.bfloat16)
    token_shape = (local_tokens, heads_all, head_size)
    head_q, head_k, head_v, head_g = (
        lax.all_to_all(scaled.reshape(token_shape), "seq", split_axis=1, concat_axis=0, tiled=True),
        lax.all_to_all(
            keys[0].reshape(token_shape), "seq", split_axis=1, concat_axis=0, tiled=True
        ),
        lax.all_to_all(
            values[0].reshape(token_shape), "seq", split_axis=1, concat_axis=0, tiled=True
        ),
        lax.all_to_all(
            grads_out[0].reshape(token_shape), "seq", split_axis=1, concat_axis=0, tiled=True
        ),
    )
    positions = jnp.arange(mesh_len, dtype=jnp.int32)
    key_valid = positions < length
    offsets = jnp.arange(stride, dtype=jnp.int32)
    whole_shape = (mesh_len, local_heads, head_size)
    zero_whole = jnp.zeros(whole_shape, jnp.float32)

    def block_rows(source, start):
        return lax.dynamic_slice_in_dim(source, start, stride, 0)

    def row_mask(start):
        return (start + offsets < length).astype(jnp.float32)

    def guarded(compute_block):
        result = compute_block(0)
        return result

    attended_all = jnp.zeros(whole_shape, jnp.bfloat16)
    dscaled_all = jnp.zeros(whole_shape, jnp.bfloat16)
    all_tops = jnp.zeros((local_heads, mesh_len, 1), jnp.float32)
    all_totals = jnp.ones((local_heads, mesh_len, 1), jnp.float32)

    def forward_step(block_index, running):
        attended_acc, tops_acc, totals_acc = running
        start = block_index * stride

        def compute_block(unused):
            scores = block_scores(block_rows(head_q, start), head_k, key_valid, inverse)
            top = jnp.max(scores, axis=2, keepdims=True)
            expo = jnp.exp(scores - top)
            total = jnp.sum(expo, axis=2, keepdims=True)
            weights_b = (expo / total).astype(jnp.bfloat16)
            return (block_output(weights_b, head_v, row_mask(start)), top, total)

        attended, top, total = guarded(compute_block)
        return (
            lax.dynamic_update_slice_in_dim(attended_acc, attended, start, 0),
            lax.dynamic_update_slice_in_dim(tops_acc, top, start, 1),
            lax.dynamic_update_slice_in_dim(totals_acc, total, start, 1),
        )

    attended_all, all_tops, all_totals = lax.fori_loop(
        0, blocks_count, forward_step, (attended_all, all_tops, all_totals)
    )
    back_attended = lax.all_to_all(attended_all, "seq", split_axis=0, concat_axis=1, tiled=True)

    def backward_step(block_index, running):
        dscaled_acc, dkeys_acc, dvalues_acc = running
        start = block_index * stride

        def compute_block(unused):
            scaled_rows = block_rows(head_q, start)
            scores = block_scores(scaled_rows, head_k, key_valid, inverse)
            top = lax.dynamic_slice_in_dim(all_tops, start, stride, 1)
            total = lax.dynamic_slice_in_dim(all_totals, start, stride, 1)
            weights = jnp.exp(scores - top) / total
            weights_b = weights.astype(jnp.bfloat16)
            return block_grads(
                scaled_rows,
                head_k,
                head_v,
                block_rows(head_g, start),
                weights,
                weights_b,
                row_mask(start),
                inverse,
            )

        dscaled, dkeys, dvalues = guarded(compute_block)
        return (
            lax.dynamic_update_slice_in_dim(dscaled_acc, dscaled, start, 0),
            dkeys_acc + dkeys,
            dvalues_acc + dvalues,
        )

    dscaled_all, dkeys_acc, dvalues_acc = lax.fori_loop(
        0, blocks_count, backward_step, (dscaled_all, zero_whole, zero_whole)
    )
    back_dscaled, back_dkeys, back_dvalues = (
        lax.all_to_all(dscaled_all, "seq", split_axis=0, concat_axis=1, tiled=True),
        lax.all_to_all(
            dkeys_acc.astype(jnp.bfloat16), "seq", split_axis=0, concat_axis=1, tiled=True
        ),
        lax.all_to_all(
            dvalues_acc.astype(jnp.bfloat16), "seq", split_axis=0, concat_axis=1, tiled=True
        ),
    )
    out_shape = (1, local_tokens, width)
    dscaled_flat = back_dscaled.reshape(local_tokens, width).astype(jnp.float32)
    query_grad = (dscaled_flat * scale_row).astype(jnp.bfloat16)
    scale_term = jnp.sum(dscaled_flat * queries[0].astype(jnp.float32), axis=0).reshape(
        heads_all, head_size
    )
    scale_grad = lax.psum(scale_term, ("dp", "seq"))
    return (
        back_attended.reshape(out_shape),
        query_grad.reshape(out_shape),
        back_dkeys.reshape(out_shape),
        back_dvalues.reshape(out_shape),
        scale_grad,
    )


def solution(mesh):
    return jax.shard_map(
        per_device,
        mesh=mesh,
        in_specs=(
            P("dp", "seq", None),
            P("dp", "seq", None),
            P("dp", "seq", None),
            P("dp", "seq", None),
            P(),
            P("dp"),
        ),
        out_specs=(
            P("dp", "seq", None),
            P("dp", "seq", None),
            P("dp", "seq", None),
            P("dp", "seq", None),
            P(),
        ),
        check_vma=False,
    )
```

profile of v0, /device:TPU:1, one launch (start us, length us, event | category | flops | bytes accessed | tf_op | source)
XLA Modules:
  0.0 356.7 jit_solution(16213372462165197923)
XLA Ops:
  0.7 1.4 copy.67
  2.1 1.0 copy-done.6
  3.1 1.8 multiply_convert_fusion.2
  4.9 10.2 %all-to-all-start = ((bf16[128,16,128]{0,2,1:T(8,128)(2,1)}), bf16[128,16,128]{0,2,1:T(8,128)(2,1)S(1)}, u32[]{:S(2)}, u32[]{:S(2)}) async-start(bf16[128,16,128]{0,2,1:T(8,128)(2,1)} %multiply_convert_fusion.2), calls=%async_computation | async-start | bytes 1048576 | tf_op jit(solution)/shard_map/all_to_all | solution.py:61
  15.2 1.0 copy.71
  16.2 14.2 %all-to-all-done = bf16[128,16,128]{0,2,1:T(8,128)(2,1)S(1)} async-done(((bf16[128,16,128]{0,2,1:T(8,128)(2,1)}), bf16[128,16,128]{0,2,1:T(8,128)(2,1)S(1)}, u32[]{:S(2)}, u32[]{:S(2)}) %all-to-all-start) | async-done | bytes 524320 | tf_op jit(solution)/shard_map/all_to_all | solution.py:61
  30.4 6.0 %all-to-all-start.2 = ((bf16[128,16,128]{0,2,1:T(8,128)(2,1)}), bf16[128,16,128]{0,2,1:T(8,128)(2,1)S(1)}, u32[]{:S(2)}, u32[]{:S(2)}) async-start(bf16[128,16,128]{0,2,1:T(8,128)(2,1)} %bitcast.8), calls=%async_computation.2 | async-start | bytes 1048576 | tf_op jit(solution)/shard_map/all_to_all | solution.py:65
  36.4 1.0 copy.69
  37.4 13.1 %all-to-all-done.2 = bf16[128,16,128]{0,2,1:T(8,128)(2,1)S(1)} async-done(((bf16[128,16,128]{0,2,1:T(8,128)(2,1)}), bf16[128,16,128]{0,2,1:T(8,128)(2,1)S(1)}, u32[]{:S(2)}, u32[]{:S(2)}) %all-to-all-start.2) | async-done | bytes 524320 | tf_op jit(solution)/shard_map/all_to_all | solution.py:65
  50.5 6.3 %all-to-all-start.1 = ((bf16[128,16,128]{0,2,1:T(8,128)(2,1)}), bf16[128,16,128]{0,2,1:T(8,128)(2,1)S(1)}, u32[]{:S(2)}, u32[]{:S(2)}) async-start(bf16[128,16,128]{0,2,1:T(8,128)(2,1)} %bitcast.4), calls=%async_computation.1 | async-start | bytes 1048576 | tf_op jit(solution)/shard_map/all_to_all | solution.py:62
  56.9 2.0 copy.75
  59.5 11.5 %all-to-all-done.1 = bf16[128,16,128]{0,2,1:T(8,128)(2,1)S(1)} async-done(((bf16[128,16,128]{0,2,1:T(8,128)(2,1)}), bf16[128,16,128]{0,2,1:T(8,128)(2,1)S(1)}, u32[]{:S(2)}, u32[]{:S(2)}) %all-to-all-start.1) | async-done | bytes 524320 | tf_op jit(solution)/shard_map/all_to_all | solution.py:62
  71.0 6.4 %all-to-all-start.4 = ((bf16[128,16,128]{0,2,1:T(8,128)(2,1)}), bf16[128,16,128]{0,2,1:T(8,128)(2,1)S(1)}, u32[]{:S(2)}, u32[]{:S(2)}) async-start(bf16[128,16,128]{0,2,1:T(8,128)(2,1)} %bitcast.15), calls=%async_computation.4 | async-start | bytes 1048576 | tf_op jit(solution)/shard_map/all_to_all | solution.py:68
  77.5 1.3 copy.70
  79.7 19.8 %while.39 = (s32[]{:T(128)}, bf16[2048,1,128]{2,0,1:T(8,128)(2,1)}, f32[1,2048,1]{1,2,0:T(1,128)S(1)}, f32[1,2048,1]{1,2,0:T(1,128)S(1)}, bf16[2048,1,128]{2,0,1...) while((s32[]{:T(128)}, bf16[2048,1,128]{2,0,1:T(8,128)(2,1)}, ...), condition=%wide.region_3.4_spmd.clone.clone, body=%wide.region_0.3_spmd.clone.clone.sunk | while | flops 549587456 | bytes 13924539 | solution.py:112
  82.8 1.8 fusion.74
  87.8 1.8 fusion.74
  92.7 1.8 fusion.74
  97.6 1.8 fusion.74
  100.3 1.3 copy.76
  102.4 53.1 %while.40 = (s32[]{:T(128)}, bf16[2048,1,128]{2,0,1:T(8,128)(2,1)}, f32[2048,1,128]{0,2,1:T(8,128)S(1)}, f32[2048,1,128]{0,2,1:T(8,128)}, bf16[2048,1,128]{2,0,1...) while((s32[]{:T(128)}, bf16[2048,1,128]{2,0,1:T(8,128)(2,1)}, ...), condition=%wide.region_6.7_spmd.clone.clone.clone, body=%wide.region_4.6_spmd.clone.clone.clone.sunk | while | flops 1354632704 | bytes 88235528 | solution.py:146
  104.6 1.6 multiply_reduce_fusion.2
  106.3 1.9 copy-done
  108.7 1.6 fusion.85
  110.3 2.4 fusion.84
  112.8 2.6 fusion.86
  117.6 1.6 multiply_reduce_fusion.2
  119.3 1.9 copy-done
  121.7 1.7 fusion.85
  123.3 2.4 fusion.84
  125.8 3.0 fusion.86
  131.0 1.6 multiply_reduce_fusion.2
  132.7 1.9 copy-done
  135.1 1.7 fusion.85
  136.7 2.4 fusion.84
  139.2 3.0 fusion.86
  144.4 1.6 multiply_reduce_fusion.2
  146.1 1.9 copy-done
  148.4 1.7 fusion.85
  150.1 2.4 fusion.84
  152.5 3.0 fusion.86
  156.1 2.1 reduce.15
  159.1 9.1 %all-to-all-start.5 = ((bf16[16,2,8192]{2,1,0:T(2,128)(2,1)}), bf16[16,2,8192]{2,1,0:T(2,128)(2,1)S(1)}, u32[]{:S(2)}, u32[]{:S(2)}) async-start(bf16[16,2,8192]{2,1,0:T(2,128)(2,1)} %reshape.268), calls=%async_computation.5 | async-start | bytes 1048576 | tf_op jit(solution)/shard_map/all_to_all | solution.py:150
  168.2 1.0 reduce.16
  170.4 11.6 %all-to-all-done.5 = bf16[16,2,8192]{2,1,0:T(2,128)(2,1)S(1)} async-done(((bf16[16,2,8192]{2,1,0:T(2,128)(2,1)}), bf16[16,2,8192]{2,1,0:T(2,128)(2,1)S(1)}, u32[]{:S(2)}, u32[]{:S(2)}) %all-to-all-start.5) | async-done | bytes 524320 | tf_op jit(solution)/shard_map/all_to_all | solution.py:150
  181.9 6.7 %all-to-all-start.6 = ((bf16[16,2,8192]{2,1,0:T(2,128)(2,1)}), bf16[16,2,8192]{2,1,0:T(2,128)(2,1)S(1)}, u32[]{:S(2)}, u32[]{:S(2)}) async-start(bf16[16,2,8192]{2,1,0:T(2,128)(2,1)} %reshape.270), calls=%async_computation.6 | async-start | bytes 1048576 | tf_op jit(solution)/shard_map/all_to_all | solution.py:151
  188.7 1.3 convert_element_type.157
  190.0 1.0 reduce.17
  192.2 10.7 %all-to-all-done.6 = bf16[16,2,8192]{2,1,0:T(2,128)(2,1)S(1)} async-done(((bf16[16,2,8192]{2,1,0:T(2,128)(2,1)}), bf16[16,2,8192]{2,1,0:T(2,128)(2,1)S(1)}, u32[]{:S(2)}, u32[]{:S(2)}) %all-to-all-start.6) | async-done | bytes 524320 | tf_op jit(solution)/shard_map/all_to_all | solution.py:151
  202.9 6.3 %all-to-all-start.7 = ((bf16[16,2,8192]{2,1,0:T(2,128)(2,1)}), bf16[16,2,8192]{2,1,0:T(2,128)(2,1)S(1)}, u32[]{:S(2)}, u32[]{:S(2)}) async-start(bf16[16,2,8192]{2,1,0:T(2,128)(2,1)} %reshape.272), calls=%async_computation.7 | async-start | bytes 1048576 | tf_op jit(solution)/shard_map/all_to_all | solution.py:154
  209.3 2.1 reduce.14
  212.2 11.3 %all-to-all-done.7 = bf16[16,2,8192]{2,1,0:T(2,128)(2,1)S(1)} async-done(((bf16[16,2,8192]{2,1,0:T(2,128)(2,1)}), bf16[16,2,8192]{2,1,0:T(2,128)(2,1)S(1)}, u32[]{:S(2)}, u32[]{:S(2)}) %all-to-all-start.7) | async-done | bytes 524320 | tf_op jit(solution)/shard_map/all_to_all | solution.py:154
  224.3 6.4 %all-to-all-start.3 = ((bf16[16,2,8192]{2,1,0:T(2,128)(2,1)}), bf16[16,2,8192]{2,1,0:T(2,128)(2,1)}, u32[]{:S(2)}, u32[]{:S(2)}) async-start(bf16[16,2,8192]{2,1,0:T(2,128)(2,1)} %reshape.266), calls=%async_computation.3 | async-start | bytes 1048576 | tf_op jit(solution)/shard_map/all_to_all | solution.py:115
  231.2 1.1 convert_element_type.167
  232.7 1.3 copy.87
  234.0 2.2 reshape.271
  237.1 1.3 copy.81
  238.4 1.0 copy.85
  239.4 2.2 reshape.273
  242.5 2.0 copy.83
  244.6 2.1 copy.86
  247.1 105.1 %psum.7 = f32[16,128]{1,0:T(8,128)} all-reduce(f32[16,128]{1,0:T(8,128)S(1)} %fusion.50), channel_id=1, replica_groups=mesh['dp'=32,'seq'=16] {'dp','seq'}, use_global_device_ids=true, to_apply=%region_8.9 | all-reduce | flops 2048 | bytes 16384 | tf_op jit(solution)/shard_map/psum | solution.py:164
  352.2 2.2 reshape.267
  354.8 1.0 copy.84
  (162 shorter events, 35.7 us)
Async XLA Ops:
  0.6 14.5 %copy-start.17 = (bf16[1,128,2048]{2,1,0:T(8,128)(2,1)S(1)}, bf16[1,128,2048]{2,1,0:T(8,128)(2,1)}, u32[]{:S(2)}) copy-start(bf16[1,128,2048]{2,1,0:T(8,128)(2,1)} %param.12) | copy-start | bytes 1572868
  0.6 35.7 %copy-start.18 = (bf16[1,128,2048]{2,1,0:T(8,128)(2,1)S(1)}, bf16[1,128,2048]{2,1,0:T(8,128)(2,1)}, u32[]{:S(2)}) copy-start(bf16[1,128,2048]{2,1,0:T(8,128)(2,1)} %param.11) | copy-start | bytes 1572868
  2.1 1.0 copy-start.6
  4.9 25.5 %all-to-all-start = ((bf16[128,16,128]{0,2,1:T(8,128)(2,1)}), bf16[128,16,128]{0,2,1:T(8,128)(2,1)S(1)}, u32[]{:S(2)}, u32[]{:S(2)}) async-start(bf16[128,16,128]{0,2,1:T(8,128)(2,1)} %multiply_convert_fusion.2), calls=%async_computation | async-start | bytes 1048576 | tf_op jit(solution)/shard_map/all_to_all | solution.py:61
  30.4 20.1 %all-to-all-start.2 = ((bf16[128,16,128]{0,2,1:T(8,128)(2,1)}), bf16[128,16,128]{0,2,1:T(8,128)(2,1)S(1)}, u32[]{:S(2)}, u32[]{:S(2)}) async-start(bf16[128,16,128]{0,2,1:T(8,128)(2,1)} %bitcast.8), calls=%async_computation.2 | async-start | bytes 1048576 | tf_op jit(solution)/shard_map/all_to_all | solution.py:65
  50.5 20.5 %all-to-all-start.1 = ((bf16[128,16,128]{0,2,1:T(8,128)(2,1)}), bf16[128,16,128]{0,2,1:T(8,128)(2,1)S(1)}, u32[]{:S(2)}, u32[]{:S(2)}) async-start(bf16[128,16,128]{0,2,1:T(8,128)(2,1)} %bitcast.4), calls=%async_computation.1 | async-start | bytes 1048576 | tf_op jit(solution)/shard_map/all_to_all | solution.py:62
  71.0 6.4 %copy-start.16 = (bf16[128,16,128]{0,2,1:T(8,128)(2,1)}, bf16[128,16,128]{0,2,1:T(8,128)(2,1)S(1)}, u32[]{:S(2)}) copy-start(bf16[128,16,128]{0,2,1:T(8,128)(2,1)S(1)} %all-to-all-done.1) | copy-start | bytes 1572868
  71.0 28.4 %all-to-all-start.4 = ((bf16[128,16,128]{0,2,1:T(8,128)(2,1)}), bf16[128,16,128]{0,2,1:T(8,128)(2,1)S(1)}, u32[]{:S(2)}, u32[]{:S(2)}) async-start(bf16[128,16,128]{0,2,1:T(8,128)(2,1)} %bitcast.15), calls=%async_computation.4 | async-start | bytes 1048576 | tf_op jit(solution)/shard_map/all_to_all | solution.py:68
  99.5 0.8 copy-start.15
  102.4 3.8 %copy-start.2 = (bf16[2048,1,128]{2,0,1:T(8,128)(2,1)}, bf16[2048,1,128]{2,0,1:T(8,128)(2,1)S(1)}, u32[]{:S(2)}) copy-start(bf16[2048,1,128]{2,0,1:T(8,128)(2,1)S(1)} %get-tuple-element.794) | copy-start | bytes 1572868 | tf_op jit(solution)/shard_map/while
  102.4 3.8 %copy-start.4 = (bf16[2048,1,128]{2,0,1:T(8,128)(2,1)}, bf16[2048,1,128]{2,0,1:T(8,128)(2,1)S(1)}, u32[]{:S(2)}) copy-start(bf16[2048,1,128]{2,0,1:T(8,128)(2,1)S(1)} %get-tuple-element.799) | copy-start | bytes 1572868 | tf_op jit(solution)/shard_map/while
  102.4 3.8 %copy-start.8 = (bf16[2048,1,128]{2,0,1:T(8,128)(2,1)}, bf16[2048,1,128]{2,0,1:T(8,128)(2,1)S(1)}, u32[]{:S(2)}) copy-start(bf16[2048,1,128]{2,0,1:T(8,128)(2,1)S(1)} %get-tuple-element.793) | copy-start | bytes 1572868 | tf_op jit(solution)/shard_map/while
  102.4 3.8 %copy-start.10 = (bf16[2048,1,128]{2,0,1:T(8,128)(2,1)}, bf16[2048,1,128]{2,0,1:T(8,128)(2,1)S(1)}, u32[]{:S(2)}) copy-start(bf16[2048,1,128]{2,0,1:T(8,128)(2,1)S(1)} %get-tuple-element.797) | copy-start | bytes 1572868 | tf_op jit(solution)/shard_map/while
  106.3 2.0 copy-start
  108.6 4.1 %copy-start.1 = (f32[512,2048]{1,0:T(8,128)S(1)}, f32[512,2048]{1,0:T(8,128)}, u32[]{:S(2)}) copy-start(f32[512,2048]{1,0:T(8,128)} %copy-done) | copy-start | bytes 12582916 | tf_op jit(solution)/shard_map/while
  112.7 2.6 copy-start.3
  112.7 2.6 copy-start.5
  112.7 2.6 copy-start.9
  112.7 2.6 copy-start.11
  115.4 3.8 %copy-start.2 = (bf16[2048,1,128]{2,0,1:T(8,128)(2,1)}, bf16[2048,1,128]{2,0,1:T(8,128)(2,1)S(1)}, u32[]{:S(2)}) copy-start(bf16[2048,1,128]{2,0,1:T(8,128)(2,1)S(1)} %get-tuple-element.794) | copy-start | bytes 1572868 | tf_op jit(solution)/shard_map/while
  115.4 3.8 %copy-start.4 = (bf16[2048,1,128]{2,0,1:T(8,128)(2,1)}, bf16[2048,1,128]{2,0,1:T(8,128)(2,1)S(1)}, u32[]{:S(2)}) copy-start(bf16[2048,1,128]{2,0,1:T(8,128)(2,1)S(1)} %get-tuple-element.799) | copy-start | bytes 1572868 | tf_op jit(solution)/shard_map/while
  115.4 3.8 %copy-start.8 = (bf16[2048,1,128]{2,0,1:T(8,128)(2,1)}, bf16[2048,1,128]{2,0,1:T(8,128)(2,1)S(1)}, u32[]{:S(2)}) copy-start(bf16[2048,1,128]{2,0,1:T(8,128)(2,1)S(1)} %get-tuple-element.793) | copy-start | bytes 1572868 | tf_op jit(solution)/shard_map/while
  115.4 3.8 %copy-start.10 = (bf16[2048,1,128]{2,0,1:T(8,128)(2,1)}, bf16[2048,1,128]{2,0,1:T(8,128)(2,1)S(1)}, u32[]{:S(2)}) copy-start(bf16[2048,1,128]{2,0,1:T(8,128)(2,1)S(1)} %get-tuple-element.797) | copy-start | bytes 1572868 | tf_op jit(solution)/shard_map/while
  119.3 2.0 copy-start
  121.7 4.1 %copy-start.1 = (f32[512,2048]{1,0:T(8,128)S(1)}, f32[512,2048]{1,0:T(8,128)}, u32[]{:S(2)}) copy-start(f32[512,2048]{1,0:T(8,128)} %copy-done) | copy-start | bytes 12582916 | tf_op jit(solution)/shard_map/while
  125.7 3.0 copy-start.3
  125.7 3.0 copy-start.5
  125.7 3.0 copy-start.9
  125.7 3.0 copy-start.11
  128.8 3.8 %copy-start.2 = (bf16[2048,1,128]{2,0,1:T(8,128)(2,1)}, bf16[2048,1,128]{2,0,1:T(8,128)(2,1)S(1)}, u32[]{:S(2)}) copy-start(bf16[2048,1,128]{2,0,1:T(8,128)(2,1)S(1)} %get-tuple-element.794) | copy-start | bytes 1572868 | tf_op jit(solution)/shard_map/while
  128.8 3.8 %copy-start.4 = (bf16[2048,1,128]{2,0,1:T(8,128)(2,1)}, bf16[2048,1,128]{2,0,1:T(8,128)(2,1)S(1)}, u32[]{:S(2)}) copy-start(bf16[2048,1,128]{2,0,1:T(8,128)(2,1)S(1)} %get-tuple-element.799) | copy-start | bytes 1572868 | tf_op jit(solution)/shard_map/while
  128.8 3.8 %copy-start.8 = (bf16[2048,1,128]{2,0,1:T(8,128)(2,1)}, bf16[2048,1,128]{2,0,1:T(8,128)(2,1)S(1)}, u32[]{:S(2)}) copy-start(bf16[2048,1,128]{2,0,1:T(8,128)(2,1)S(1)} %get-tuple-element.793) | copy-start | bytes 1572868 | tf_op jit(solution)/shard_map/while
  128.8 3.8 %copy-start.10 = (bf16[2048,1,128]{2,0,1:T(8,128)(2,1)}, bf16[2048,1,128]{2,0,1:T(8,128)(2,1)S(1)}, u32[]{:S(2)}) copy-start(bf16[2048,1,128]{2,0,1:T(8,128)(2,1)S(1)} %get-tuple-element.797) | copy-start | bytes 1572868 | tf_op jit(solution)/shard_map/while
  132.7 2.0 copy-start
  135.0 4.1 %copy-start.1 = (f32[512,2048]{1,0:T(8,128)S(1)}, f32[512,2048]{1,0:T(8,128)}, u32[]{:S(2)}) copy-start(f32[512,2048]{1,0:T(8,128)} %copy-done) | copy-start | bytes 12582916 | tf_op jit(solution)/shard_map/while
  139.1 3.0 copy-start.3
  139.1 3.0 copy-start.5
  139.1 3.0 copy-start.9
  139.1 3.0 copy-start.11
  142.2 3.8 %copy-start.2 = (bf16[2048,1,128]{2,0,1:T(8,128)(2,1)}, bf16[2048,1,128]{2,0,1:T(8,128)(2,1)S(1)}, u32[]{:S(2)}) copy-start(bf16[2048,1,128]{2,0,1:T(8,128)(2,1)S(1)} %get-tuple-element.794) | copy-start | bytes 1572868 | tf_op jit(solution)/shard_map/while
  142.2 3.8 %copy-start.4 = (bf16[2048,1,128]{2,0,1:T(8,128)(2,1)}, bf16[2048,1,128]{2,0,1:T(8,128)(2,1)S(1)}, u32[]{:S(2)}) copy-start(bf16[2048,1,128]{2,0,1:T(8,128)(2,1)S(1)} %get-tuple-element.799) | copy-start | bytes 1572868 | tf_op jit(solution)/shard_map/while
  142.2 3.8 %copy-start.8 = (bf16[2048,1,128]{2,0,1:T(8,128)(2,1)}, bf16[2048,1,128]{2,0,1:T(8,128)(2,1)S(1)}, u32[]{:S(2)}) copy-start(bf16[2048,1,128]{2,0,1:T(8,128)(2,1)S(1)} %get-tuple-element.793) | copy-start | bytes 1572868 | tf_op jit(solution)/shard_map/while
  142.2 3.8 %copy-start.10 = (bf16[2048,1,128]{2,0,1:T(8,128)(2,1)}, bf16[2048,1,128]{2,0,1:T(8,128)(2,1)S(1)}, u32[]{:S(2)}) copy-start(bf16[2048,1,128]{2,0,1:T(8,128)(2,1)S(1)} %get-tuple-element.797) | copy-start | bytes 1572868 | tf_op jit(solution)/shard_map/while
  146.0 2.0 copy-start
  148.4 4.1 %copy-start.1 = (f32[512,2048]{1,0:T(8,128)S(1)}, f32[512,2048]{1,0:T(8,128)}, u32[]{:S(2)}) copy-start(f32[512,2048]{1,0:T(8,128)} %copy-done) | copy-start | bytes 12582916 | tf_op jit(solution)/shard_map/while
  152.5 3.0 copy-start.3
  152.5 3.0 copy-start.5
  152.5 3.0 copy-start.9
  152.5 3.0 copy-start.11
  159.1 22.9 %all-to-all-start.5 = ((bf16[16,2,8192]{2,1,0:T(2,128)(2,1)}), bf16[16,2,8192]{2,1,0:T(2,128)(2,1)S(1)}, u32[]{:S(2)}, u32[]{:S(2)}) async-start(bf16[16,2,8192]{2,1,0:T(2,128)(2,1)} %reshape.268), calls=%async_computation.5 | async-start | bytes 1048576 | tf_op jit(solution)/shard_map/all_to_all | solution.py:150
  181.9 21.0 %all-to-all-start.6 = ((bf16[16,2,8192]{2,1,0:T(2,128)(2,1)}), bf16[16,2,8192]{2,1,0:T(2,128)(2,1)S(1)}, u32[]{:S(2)}, u32[]{:S(2)}) async-start(bf16[16,2,8192]{2,1,0:T(2,128)(2,1)} %reshape.270), calls=%async_computation.6 | async-start | bytes 1048576 | tf_op jit(solution)/shard_map/all_to_all | solution.py:151
  202.9 20.6 %copy-start.13 = (bf16[16,2,8192]{2,1,0:T(2,128)(2,1)}, bf16[16,2,8192]{2,1,0:T(2,128)(2,1)S(1)}, u32[]{:S(2)}) copy-start(bf16[16,2,8192]{2,1,0:T(2,128)(2,1)S(1)} %all-to-all-done.6) | copy-start | bytes 1572868
  202.9 20.6 %all-to-all-start.7 = ((bf16[16,2,8192]{2,1,0:T(2,128)(2,1)}), bf16[16,2,8192]{2,1,0:T(2,128)(2,1)S(1)}, u32[]{:S(2)}, u32[]{:S(2)}) async-start(bf16[16,2,8192]{2,1,0:T(2,128)(2,1)} %reshape.272), calls=%async_computation.7 | async-start | bytes 1048576 | tf_op jit(solution)/shard_map/all_to_all | solution.py:154
  223.5 0.8 copy-start.14
  224.3 127.9 %all-to-all-start.3 = ((bf16[16,2,8192]{2,1,0:T(2,128)(2,1)}), bf16[16,2,8192]{2,1,0:T(2,128)(2,1)}, u32[]{:S(2)}, u32[]{:S(2)}) async-start(bf16[16,2,8192]{2,1,0:T(2,128)(2,1)} %reshape.266), calls=%async_computation.3 | async-start | bytes 1048576 | tf_op jit(solution)/shard_map/all_to_all | solution.py:115
  236.2 10.5 %copy-start.7 = (f32[1,128,2048]{1,2,0:T(8,128)S(1)}, f32[1,128,2048]{1,2,0:T(8,128)}, u32[]{:S(2)}) copy-start(f32[1,128,2048]{1,2,0:T(8,128)} %copy-done.6) | copy-start | bytes 3145732
  244.6 111.2 %copy-start.12 = (f32[1,128,2048]{2,1,0:T(8,128)S(1)}, f32[1,128,2048]{2,1,0:T(8,128)}, u32[]{:S(2)}) copy-start(f32[1,128,2048]{2,1,0:T(8,128)} %copy.87) | copy-start | bytes 3145732
  244.6 111.2 %copy-start.19 = (f32[16,128]{1,0:T(8,128)S(1)}, f32[16,128]{1,0:T(8,128)}, u32[]{:S(2)}) copy-start(f32[16,128]{1,0:T(8,128)} %param.14) | copy-start | bytes 24580
where the time goes:
time: 358 us; the launch traced here: 357 us
  blocking collectives  105 us (29%)
  waiting for transfers between devices  72.4 us (20%)
  starting transfers between devices  57.4 us (16%)
  matrix products  48.1 us (13%)
  local copies, waits for them, and re-layouts  44.1 us (12%)
  other arithmetic  27.8 us (8%)
    psum x1, blocking collectives, per_device(): scale_grad = lax.psum(scale_term, ('dp', 'seq'))  105 us
    unnamed x40, local copies, waits for them, and re-layouts  25.4 us
    all_to_all x1, waiting for transfers between devices, per_device(): lax.all_to_all(scaled.reshape(token_shape), 'seq', split_axis=1, concat_a...  14.2 us
    all_to_all x1, waiting for transfers between devices, per_device(): lax.all_to_all(values[0].reshape(token_shape), 'seq', split_axis=1, conca...  13.1 us
    dot_general x4, matrix products, block_grads(): jnp.einsum('gqk,qgd->kgd', weights_b, masked, preferred_element_type=jnp....  11.6 us
    all_to_all x1, waiting for transfers between devices, per_device(): lax.all_to_all(dscaled_all, 'seq', split_axis=0, concat_axis=1, tiled=True)  11.6 us
    all_to_all x1, waiting for transfers between devices, per_device(): lax.all_to_all(keys[0].reshape(token_shape), 'seq', split_axis=1, concat_...  11.5 us
    all_to_all x1, waiting for transfers between devices, per_device(): lax.all_to_all(dvalues_acc.astype(jnp.bfloat16), 'seq', split_axis=0, con...  11.3 us
  transfers between devices with their start and end apart: 8, of which 6 were waited for; matrix products, arithmetic and copies ran while one was open for 14% of the time, Pallas kernels for 0%

commit v1 on v0

v1 whole, which is shorter than its diff:
```python
import functools
import math

import jax
import jax.numpy as jnp
from jax import lax
from jax.experimental import pallas as pl
from jax.experimental.pallas import tpu as pltpu
from jax.sharding import Mesh, PartitionSpec as P

f32 = jnp.float32
bf16 = jnp.bfloat16
NEG = -1e30
BLOCK_Q = 512
BLOCK_K = 1024
ALONG_ROWS = (((1,), (1,)), ((), ()))
PLAIN = (((1,), (0,)), ((), ()))
VMEM = pl.BlockSpec(memory_space=pltpu.VMEM)
SMEM = pl.BlockSpec(memory_space=pltpu.SMEM)


def dot(a, b, dims=PLAIN):
    return lax.dot_general(a, b, dims, preferred_element_type=f32)


def split_kernel(heads, size, *refs):
    sources, out_ref = refs[:-1], refs[-1]
    for head in range(heads):
        for place, source in enumerate(sources):
            out_ref[head, place] = source[:, head * size : (head + 1) * size]


def join_kernel(heads, size, *refs):
    source, outs = refs[0], refs[1:]
    for head in range(heads):
        for place, out in enumerate(outs):
            out[:, head * size : (head + 1) * size] = source[head, place]


def attention_kernel(
    tokens, block_q, block_k, length_ref, scale_ref, x_ref, out_ref, term_ref,
    keys_t, values_t, scores, dprobs, dkeys, dvalues,
):
    part, size = x_ref.shape[2], x_ref.shape[3]
    inverse = 1.0 / math.sqrt(size)
    factor = inverse * math.log2(math.e)
    length = length_ref[0]
    q_blocks = (length + block_q - 1) // block_q
    k_blocks = (length + block_k - 1) // block_k
    q_parts, k_parts = block_q // part, block_k // part
    scale = scale_ref[...]

    def rows_of(block, parts, operand):
        return x_ref[pl.ds(block * parts, parts), operand].reshape(parts * part, size)

    def key_rows(block):
        return pl.ds(pl.multiple_of(block * block_k, block_k), block_k)

    def fold(wide, op):
        return op(wide.reshape(block_k // 8, 8, block_q), axis=0)

    def transpose(block, carry):
        keys_t[:, key_rows(block)] = rows_of(block, k_parts, 1).T
        values_t[:, key_rows(block)] = rows_of(block, k_parts, 2).T
        return carry

    lax.fori_loop(0, k_blocks, transpose, 0)
    term_ref[...] = jnp.zeros_like(term_ref)
    dkeys[...] = jnp.zeros_like(dkeys)
    dvalues[...] = jnp.zeros_like(dvalues)

    def query_block(block, carry):
        positions = lax.broadcasted_iota(jnp.int32, (block_q, size), 0) + block * block_q
        valid = positions < length
        queries = rows_of(block, q_parts, 0).astype(f32)
        scaled = (queries * scale).astype(bf16)
        grads = jnp.where(valid, rows_of(block, q_parts, 3).astype(f32), 0.0).astype(bf16)

        def score_step(j, top):
            raw = dot(rows_of(j, k_parts, 1), scaled, ALONG_ROWS)
            places = lax.broadcasted_iota(jnp.int32, (block_k, block_q), 0) + j * block_k
            raw = jnp.where(places < length, raw, NEG)
            scores[key_rows(j), :] = raw
            return jnp.maximum(top, fold(raw, jnp.max))

        top = lax.fori_loop(0, k_blocks, score_step, jnp.full((8, block_q), NEG, f32))
        top = jnp.max(top, axis=0, keepdims=True)

        def prob_step(j, sums):
            total, weighted = sums
            dprob = dot(rows_of(j, k_parts, 2), grads, ALONG_ROWS)
            expo = jnp.exp2((scores[key_rows(j), :] - top) * factor)
            scores[key_rows(j), :] = expo
            dprobs[key_rows(j), :] = dprob
            return total + fold(expo, jnp.sum), weighted + fold(expo * dprob, jnp.sum)

        zero = jnp.zeros((8, block_q), f32)
        total, weighted = lax.fori_loop(0, k_blocks, prob_step, (zero, zero))
        share = 1.0 / jnp.sum(total, axis=0, keepdims=True)
        delta = jnp.sum(weighted, axis=0, keepdims=True) * share

        def grad_step(j, sums):
            out_t, dscaled_t = sums
            rows = key_rows(j)
            probs = scores[rows, :] * share
            probs_b = probs.astype(bf16)
            dscore = (probs * (dprobs[rows, :] - delta)).astype(bf16)
            dvalues[rows, :] += dot(probs_b, grads)
            dkeys[rows, :] += dot(dscore, scaled)
            return out_t + dot(values_t[:, rows], probs_b), dscaled_t + dot(keys_t[:, rows], dscore)

        zero = jnp.zeros((size, block_q), f32)
        out_t, dscaled_t = lax.fori_loop(0, k_blocks, grad_step, (zero, zero))
        attended = jnp.where(valid, out_t.T, 0.0).astype(bf16)
        dscaled = (dscaled_t.T * inverse).astype(bf16).astype(f32)
        term_ref[...] += jnp.sum((dscaled * queries).reshape(block_q // 8, 8, size), axis=0)
        here = pl.ds(block * q_parts, q_parts)
        out_ref[here, 0] = attended.reshape(q_parts, part, size)
        out_ref[here, 1] = (dscaled * scale).astype(bf16).reshape(q_parts, part, size)
        return carry

    lax.fori_loop(0, q_blocks, query_block, 0)

    def clear(block, carry):
        out_ref[pl.ds(block * q_parts, q_parts), 0:2] = jnp.zeros((q_parts, 2, part, size), bf16)
        return carry

    lax.fori_loop(q_blocks, tokens // block_q, clear, 0)

    def finish(j, carry):
        here, rows = pl.ds(j * k_parts, k_parts), key_rows(j)
        out_ref[here, 2] = (dkeys[rows, :] * inverse).astype(bf16).reshape(k_parts, part, size)
        out_ref[here, 3] = dvalues[rows, :].astype(bf16).reshape(k_parts, part, size)
        return carry

    lax.fori_loop(0, tokens // block_k, finish, 0)


def attend(length, scale, x):
    blocks, _, part, size = x.shape
    tokens = blocks * part
    block_q, block_k = min(BLOCK_Q, tokens), min(BLOCK_K, tokens)
    flops = 12 * tokens * tokens * size
    return pl.pallas_call(
        functools.partial(attention_kernel, tokens, block_q, block_k),
        out_shape=(
            jax.ShapeDtypeStruct(x.shape, bf16),
            jax.ShapeDtypeStruct((8, size), f32),
        ),
        in_specs=[SMEM, VMEM, VMEM],
        out_specs=(VMEM, VMEM),
        scratch_shapes=[
            pltpu.VMEM((size, tokens), bf16),
            pltpu.VMEM((size, tokens), bf16),
            pltpu.VMEM((tokens, block_q), f32),
            pltpu.VMEM((tokens, block_q), f32),
            pltpu.VMEM((tokens, size), f32),
            pltpu.VMEM((tokens, size), f32),
        ],
        cost_estimate=pl.CostEstimate(
            flops=flops, bytes_accessed=4 * x.size, transcendentals=tokens * tokens
        ),
        compiler_params=pltpu.CompilerParams(vmem_limit_bytes=40 * 1024 * 1024),
        name="attention",
    )(length, scale, x)


def swap_sum(value, axis, step):
    count = lax.axis_size(axis)
    return value + lax.ppermute(value, axis, [(i, i ^ step) for i in range(count)])


def per_device(queries, keys, values, grads_out, q_scale, lengths):
    heads, size = q_scale.shape
    local, width = queries.shape[1:]
    seq = ("xh", "y")
    me = lax.axis_index(seq)
    small = pltpu.CompilerParams(vmem_limit_bytes=16 * 1024 * 1024)
    x = pl.pallas_call(
        functools.partial(split_kernel, heads, size),
        out_shape=jax.ShapeDtypeStruct((heads, 4, local, size), bf16),
        in_specs=[VMEM] * 4,
        out_specs=VMEM,
        compiler_params=small,
        name="split",
    )(queries[0], keys[0], values[0], grads_out[0])
    x = lax.all_to_all(x, seq, 0, 0, tiled=True)
    scale = lax.dynamic_slice_in_dim(q_scale, me, 1, 0)
    results, term = attend(lengths, scale, x)
    back = lax.all_to_all(results, seq, 0, 0, tiled=True)

    term = jnp.sum(term, axis=0, keepdims=True)
    for axis, step in (("c", 1), ("xl", 1), ("z", 1), ("z", 2), ("z", 4)):
        term = swap_sum(term, axis, step)
    grid = jnp.where(lax.broadcasted_iota(jnp.int32, (heads, size), 0) == me, term, 0.0)
    for axis, step in (("xh", 1), ("y", 1), ("y", 2), ("y", 4)):
        grid = swap_sum(grid, axis, step)

    outs = pl.pallas_call(
        functools.partial(join_kernel, heads, size),
        out_shape=[jax.ShapeDtypeStruct((local, width), bf16)] * 4,
        in_specs=[VMEM],
        out_specs=[VMEM] * 4,
        compiler_params=small,
        name="join",
    )(back)
    return tuple(out[None] for out in outs) + (grid,)


def solution(mesh):
    fine = Mesh(mesh.devices.reshape(2, 8, 2, 2, 8), ("xl", "z", "c", "xh", "y"))
    tokens = P(("xl", "z", "c"), ("xh", "y"), None)
    return jax.shard_map(
        per_device,
        mesh=fine,
        in_specs=(tokens, tokens, tokens, tokens, P(), P(("xl", "z", "c"))),
        out_specs=(tokens, tokens, tokens, tokens, P()),
        check_vma=False,
    )
```

time: 358 us -> 160 us (0.45)
  the two profiles are of different devices: /device:TPU:1 before, /device:TPU:104 now
where the time goes in v1:
time: 160 us; the launch traced here: 159 us
  waiting for transfers between devices  81.7 us (51%)
  starting transfers between devices  47 us (29%)
  Pallas kernels  22.7 us (14%)
  local copies, waits for them, and re-layouts  5.52 us (3%)
    all_to_all x1, waiting for transfers between devices, per_device(): x = lax.all_to_all(x, seq, 0, 0, tiled=True)  45.4 us
    ppermute x9, waiting for transfers between devices, swap_sum(): lax.ppermute(value, axis, [(i, i ^ step) for i in range(count)])  36.3 us
    ppermute x9, starting transfers between devices, swap_sum(): lax.ppermute(value, axis, [(i, i ^ step) for i in range(count)])  27.3 us
    pallas_call x1, Pallas kernels, attend(): pl.pallas_call(functools.partial(attention_kernel, tokens, block_q, block...  19.1 us
    all_to_all x1, starting transfers between devices, per_device(): back = lax.all_to_all(results, seq, 0, 0, tiled=True)  10.1 us
    all_to_all x1, starting transfers between devices, per_device(): x = lax.all_to_all(x, seq, 0, 0, tiled=True)  9.57 us
    unnamed x12, local copies, waits for them, and re-layouts  5.5 us
  transfers between devices with their start and end apart: 11, of which 10 were waited for; matrix products, arithmetic and copies ran while one was open for 1% of the time, Pallas kernels for 0%

profile of v1, /device:TPU:104, one launch (start us, length us, event | category | flops | bytes accessed | tf_op | source)
XLA Modules:
  0.0 159.2 jit_solution(9725421531997376438)
XLA Ops:
  0.6 0.0 copy-start
  0.6 0.0 copy-start.2
  0.7 1.0 copy-done.2
  1.7 0.0 copy-start.3
  1.7 1.0 copy-done.3
  2.7 0.0 copy-start.4
  2.7 1.0 copy-done.4
  3.8 0.0 copy-start.5
  3.8 1.0 copy-done.5
  4.8 1.7 %split.1 = bf16[16,4,128,128]{3,2,1,0:T(8,128)(2,1)} custom-call(bf16[128,2048]{1,0:T(8,128)(2,1)S(1)} %bitcast.12, bf16[128,2048]{1,0:T(8,128)(2,1)S(1)} %bitcast.13, bf16[128,2048]{1,0:T(8,128)(2,1)S(1)} %bitcast.14, bf16[128,2048]{1,0:T(8,128)(2,1)S(1)} %bitcast.15), custom_call_target="tpu_custom_call" | custom-call | tf_op jit(solution)/shard_map/split/pallas_call | solution.py:179
  6.5 9.6 %all-to-all-start = ((bf16[16,4,128,128]{3,2,1,0:T(8,128)(2,1)}), bf16[16,4,128,128]{3,2,1,0:T(8,128)(2,1)S(1)}, u32[]{:S(2)}, u32[]{:S(2)}) async-start(bf16[16,4,128,128]{3,2,1,0:T(8,128)(2,1)} %split.1), calls=%async_computation | async-start | bytes 4194304 | tf_op jit(solution)/shard_map/all_to_all | solution.py:187
  16.8 0.0 copy-done
  16.8 45.4 %all-to-all-done.x_ref = bf16[16,4,128,128]{3,2,1,0:T(8,128)(2,1)S(1)} async-done(((bf16[16,4,128,128]{3,2,1,0:T(8,128)(2,1)}), bf16[16,4,128,128]{3,2,1,0:T(8,128)(2,1)S(1)}, u32[]{:S(2)}, u32[]{:S(2)}) %all-to-all-start) | async-done | bytes 2097184 | tf_op jit(solution)/shard_map/all_to_all | solution.py:187
  62.2 19.1 %attention.1 = (bf16[16,4,128,128]{3,2,1,0:T(8,128)(2,1)S(1)}, f32[8,128]{1,0:T(8,128)S(1)}) custom-call(s32[1]{0:T(128)S(6)} %copy.11.length_ref, f32[1,128]{1,0:T(1,128)S(1)} %constant_dynamic-slice_fusion.scale_ref, bf16[16,4,128,128]{3,2,1,0:T(8,128)(2,1)S(1)} %all-to-all-done.x_ref), custom_call_target="tpu_custom_call" | custom-call | flops 6442450944 | bytes 4194304 | tf_op jit(solution)/shard_map/attention/pallas_call | solution.py:144
  81.3 0.0 copy-start.1
  81.3 1.3 copy-done.1
  82.7 10.1 %all-to-all-start.1 = ((bf16[16,4,128,128]{3,2,1,0:T(8,128)(2,1)}), bf16[16,4,128,128]{3,2,1,0:T(8,128)(2,1)S(1)}, u32[]{:S(2)}, u32[]{:S(2)}) async-start(bf16[16,4,128,128]{3,2,1,0:T(8,128)(2,1)} %copy-done.1), calls=%async_computation.1 | async-start | bytes 4194304 | tf_op jit(solution)/shard_map/all_to_all | solution.py:190
  92.8 1.9 %collective-permute-start = (f32[1,128]{1,0:T(1,128)S(1)}, f32[1,128]{1,0:T(1,128)S(1)}, u32[]{:S(2)}, u32[]{:S(2)}) collective-permute-start(f32[1,128]{1,0:T(1,128)S(1)} %bitcast.16), channel_id=1, source_target_pairs={{0,16},{16,0},{1,17},{17,1},{2,18},{18,2},{3,19},{19,3},{4,20},{20... | collective-permute-start | bytes 1544 | tf_op jit(solution)/shard_map/ppermute | solution.py:170
  94.7 1.1 collective-permute-done
  95.8 1.9 %collective-permute-start.1 = (f32[1,128]{1,0:T(1,128)S(1)}, f32[1,128]{1,0:T(1,128)S(1)}, u32[]{:S(2)}, u32[]{:S(2)}) collective-permute-start(f32[1,128]{1,0:T(1,128)S(1)} %bitcast_add_fusion), channel_id=1, source_target_pairs={{0,256},{256,0},{1,257},{257,1},{2,258},{258,2},{3,259},{259,3},{4... | collective-permute-start | bytes 1544 | tf_op jit(solution)/shard_map/ppermute | solution.py:170
  97.7 3.5 %collective-permute-done.1 = f32[1,128]{1,0:T(1,128)S(1)} collective-permute-done((f32[1,128]{1,0:T(1,128)S(1)}, f32[1,128]{1,0:T(1,128)S(1)}, u32[]{:S(2)}, u32[]{:S(2)}) %collective-permute-start.1) | collective-permute-done | bytes 544 | tf_op jit(solution)/shard_map/ppermute | solution.py:170
  101.2 1.9 %collective-permute-start.2 = (f32[1,128]{1,0:T(1,128)S(1)}, f32[1,128]{1,0:T(1,128)S(1)}, u32[]{:S(2)}, u32[]{:S(2)}) collective-permute-start(f32[1,128]{1,0:T(1,128)S(1)} %add.36), channel_id=1, source_target_pairs={{0,32},{32,0},{64,96},{96,64},{128,160},{160,128},{192,224},{224,1... | collective-permute-start | bytes 1544 | tf_op jit(solution)/shard_map/ppermute | solution.py:170
  103.1 3.5 %collective-permute-done.2 = f32[1,128]{1,0:T(1,128)S(1)} collective-permute-done((f32[1,128]{1,0:T(1,128)S(1)}, f32[1,128]{1,0:T(1,128)S(1)}, u32[]{:S(2)}, u32[]{:S(2)}) %collective-permute-start.2) | collective-permute-done | bytes 544 | tf_op jit(solution)/shard_map/ppermute | solution.py:170
  106.6 1.9 %collective-permute-start.3 = (f32[1,128]{1,0:T(1,128)S(1)}, f32[1,128]{1,0:T(1,128)S(1)}, u32[]{:S(2)}, u32[]{:S(2)}) collective-permute-start(f32[1,128]{1,0:T(1,128)S(1)} %add.37), channel_id=1, source_target_pairs={{0,64},{32,96},{64,0},{96,32},{128,192},{160,224},{192,128},{224,1... | collective-permute-start | bytes 1544 | tf_op jit(solution)/shard_map/ppermute | solution.py:170
  108.5 4.4 %collective-permute-done.3 = f32[1,128]{1,0:T(1,128)S(1)} collective-permute-done((f32[1,128]{1,0:T(1,128)S(1)}, f32[1,128]{1,0:T(1,128)S(1)}, u32[]{:S(2)}, u32[]{:S(2)}) %collective-permute-start.3) | collective-permute-done | bytes 544 | tf_op jit(solution)/shard_map/ppermute | solution.py:170
  112.9 9.1 %collective-permute-start.4 = (f32[1,128]{1,0:T(1,128)S(1)}, f32[1,128]{1,0:T(1,128)S(1)}, u32[]{:S(2)}, u32[]{:S(2)}) collective-permute-start(f32[1,128]{1,0:T(1,128)S(1)} %add.38), channel_id=1, source_target_pairs={{0,128},{32,160},{64,192},{96,224},{128,0},{160,32},{192,64},{224,... | collective-permute-start | bytes 1544 | tf_op jit(solution)/shard_map/ppermute | solution.py:170
  122.1 1.5 collective-permute-done.4
  123.6 0.1 broadcast_select_fusion
  123.6 4.9 %collective-permute-start.5 = (f32[16,128]{1,0:T(8,128)S(1)}, f32[16,128]{1,0:T(8,128)S(1)}, u32[]{:S(2)}, u32[]{:S(2)}) collective-permute-start(f32[16,128]{1,0:T(8,128)S(1)} %broadcast_select_fusion), channel_id=1, source_target_pairs={{0,8},{8,0},{1,9},{9,1},{2,10},{10,2},{3,11},{11,3},{4,12},{12,4},... | collective-permute-start | bytes 24584 | tf_op jit(solution)/shard_map/ppermute | solution.py:170
  128.5 6.6 %collective-permute-done.5 = f32[16,128]{1,0:T(8,128)S(1)} collective-permute-done((f32[16,128]{1,0:T(8,128)S(1)}, f32[16,128]{1,0:T(8,128)S(1)}, u32[]{:S(2)}, u32[]{:S(2)}) %collective-permute-start.5) | collective-permute-done | bytes 8224 | tf_op jit(solution)/shard_map/ppermute | solution.py:170
  135.2 0.1 fusion
  135.2 1.9 %collective-permute-start.6 = (f32[16,128]{1,0:T(8,128)S(1)}, f32[16,128]{1,0:T(8,128)S(1)}, u32[]{:S(2)}, u32[]{:S(2)}) collective-permute-start(f32[16,128]{1,0:T(8,128)S(1)} %fusion), channel_id=1, source_target_pairs={{0,1},{1,0},{2,3},{3,2},{4,5},{5,4},{6,7},{7,6},{8,9},{9,8},{10,11... | collective-permute-start | bytes 24584 | tf_op jit(solution)/shard_map/ppermute | solution.py:170
  137.1 3.6 %collective-permute-done.6 = f32[16,128]{1,0:T(8,128)S(1)} collective-permute-done((f32[16,128]{1,0:T(8,128)S(1)}, f32[16,128]{1,0:T(8,128)S(1)}, u32[]{:S(2)}, u32[]{:S(2)}) %collective-permute-start.6) | collective-permute-done | bytes 8224 | tf_op jit(solution)/shard_map/ppermute | solution.py:170
  140.8 0.1 fusion.1
  140.8 1.9 %collective-permute-start.7 = (f32[16,128]{1,0:T(8,128)S(1)}, f32[16,128]{1,0:T(8,128)S(1)}, u32[]{:S(2)}, u32[]{:S(2)}) collective-permute-start(f32[16,128]{1,0:T(8,128)S(1)} %fusion.1), channel_id=1, source_target_pairs={{0,2},{1,3},{2,0},{3,1},{4,6},{5,7},{6,4},{7,5},{8,10},{9,11},{10,... | collective-permute-start | bytes 24584 | tf_op jit(solution)/shard_map/ppermute | solution.py:170
  142.8 4.5 %collective-permute-done.7 = f32[16,128]{1,0:T(8,128)S(1)} collective-permute-done((f32[16,128]{1,0:T(8,128)S(1)}, f32[16,128]{1,0:T(8,128)S(1)}, u32[]{:S(2)}, u32[]{:S(2)}) %collective-permute-start.7) | collective-permute-done | bytes 8224 | tf_op jit(solution)/shard_map/ppermute | solution.py:170
  147.3 1.9 %collective-permute-start.8 = (f32[16,128]{1,0:T(8,128)S(1)}, f32[16,128]{1,0:T(8,128)S(1)}, u32[]{:S(2)}, u32[]{:S(2)}) collective-permute-start(f32[16,128]{1,0:T(8,128)S(1)} %add.42), channel_id=1, source_target_pairs={{0,4},{1,5},{2,6},{3,7},{4,0},{5,1},{6,2},{7,3},{8,12},{9,13},{10,... | collective-permute-start | bytes 24584 | tf_op jit(solution)/shard_map/ppermute | solution.py:170
  149.2 7.5 %collective-permute-done.8 = f32[16,128]{1,0:T(8,128)S(1)} collective-permute-done((f32[16,128]{1,0:T(8,128)S(1)}, f32[16,128]{1,0:T(8,128)S(1)}, u32[]{:S(2)}, u32[]{:S(2)}) %collective-permute-start.8) | collective-permute-done | bytes 8224 | tf_op jit(solution)/shard_map/ppermute | solution.py:170
  156.7 0.6 add.43
  157.3 0.0 all-to-all-done.1.refs_0_
  157.3 1.9 %join.1 = (bf16[128,2048]{1,0:T(8,128)(2,1)}, bf16[128,2048]{1,0:T(8,128)(2,1)}, bf16[128,2048]{1,0:T(8,128)(2,1)}, bf16[128,2048]{1,0:T(8,128)(2,1)}) custom-call(bf16[16,4,128,128]{3,2,1,0:T(8,128)(2,1)S(1)} %all-to-all-done.1.refs_0_), custom_call_target="tpu_custom_call" | custom-call | tf_op jit(solution)/shard_map/join/pallas_call | solution.py:199
  (9 shorter events, 0.1 us)
Async XLA Ops:
  0.6 16.1 %copy-start = (f32[16,128]{1,0:T(8,128)S(1)}, f32[16,128]{1,0:T(8,128)}, u32[]{:S(2)}) copy-start(f32[16,128]{1,0:T(8,128)} %param.10) | copy-start | bytes 24580
  0.6 1.0 copy-start.2
  1.7 1.0 copy-start.3
  2.7 1.0 copy-start.4
  3.8 1.0 copy-start.5
  6.5 55.6 %all-to-all-start = ((bf16[16,4,128,128]{3,2,1,0:T(8,128)(2,1)}), bf16[16,4,128,128]{3,2,1,0:T(8,128)(2,1)S(1)}, u32[]{:S(2)}, u32[]{:S(2)}) async-start(bf16[16,4,128,128]{3,2,1,0:T(8,128)(2,1)} %split.1), calls=%async_computation | async-start | bytes 4194304 | tf_op jit(solution)/shard_map/all_to_all | solution.py:187
  81.3 1.3 copy-start.1
  82.7 74.7 %all-to-all-start.1 = ((bf16[16,4,128,128]{3,2,1,0:T(8,128)(2,1)}), bf16[16,4,128,128]{3,2,1,0:T(8,128)(2,1)S(1)}, u32[]{:S(2)}, u32[]{:S(2)}) async-start(bf16[16,4,128,128]{3,2,1,0:T(8,128)(2,1)} %copy-done.1), calls=%async_computation.1 | async-start | bytes 4194304 | tf_op jit(solution)/shard_map/all_to_all | solution.py:190
  92.8 3.0 %collective-permute-start = (f32[1,128]{1,0:T(1,128)S(1)}, f32[1,128]{1,0:T(1,128)S(1)}, u32[]{:S(2)}, u32[]{:S(2)}) collective-permute-start(f32[1,128]{1,0:T(1,128)S(1)} %bitcast.16), channel_id=1, source_target_pairs={{0,16},{16,0},{1,17},{17,1},{2,18},{18,2},{3,19},{19,3},{4,20},{20... | collective-permute-start | bytes 1544 | tf_op jit(solution)/shard_map/ppermute | solution.py:170
  95.8 5.4 %collective-permute-start.1 = (f32[1,128]{1,0:T(1,128)S(1)}, f32[1,128]{1,0:T(1,128)S(1)}, u32[]{:S(2)}, u32[]{:S(2)}) collective-permute-start(f32[1,128]{1,0:T(1,128)S(1)} %bitcast_add_fusion), channel_id=1, source_target_pairs={{0,256},{256,0},{1,257},{257,1},{2,258},{258,2},{3,259},{259,3},{4... | collective-permute-start | bytes 1544 | tf_op jit(solution)/shard_map/ppermute | solution.py:170
  101.2 5.4 %collective-permute-start.2 = (f32[1,128]{1,0:T(1,128)S(1)}, f32[1,128]{1,0:T(1,128)S(1)}, u32[]{:S(2)}, u32[]{:S(2)}) collective-permute-start(f32[1,128]{1,0:T(1,128)S(1)} %add.36), channel_id=1, source_target_pairs={{0,32},{32,0},{64,96},{96,64},{128,160},{160,128},{192,224},{224,1... | collective-permute-start | bytes 1544 | tf_op jit(solution)/shard_map/ppermute | solution.py:170
  106.6 6.3 %collective-permute-start.3 = (f32[1,128]{1,0:T(1,128)S(1)}, f32[1,128]{1,0:T(1,128)S(1)}, u32[]{:S(2)}, u32[]{:S(2)}) collective-permute-start(f32[1,128]{1,0:T(1,128)S(1)} %add.37), channel_id=1, source_target_pairs={{0,64},{32,96},{64,0},{96,32},{128,192},{160,224},{192,128},{224,1... | collective-permute-start | bytes 1544 | tf_op jit(solution)/shard_map/ppermute | solution.py:170
  112.9 10.6 %collective-permute-start.4 = (f32[1,128]{1,0:T(1,128)S(1)}, f32[1,128]{1,0:T(1,128)S(1)}, u32[]{:S(2)}, u32[]{:S(2)}) collective-permute-start(f32[1,128]{1,0:T(1,128)S(1)} %add.38), channel_id=1, source_target_pairs={{0,128},{32,160},{64,192},{96,224},{128,0},{160,32},{192,64},{224,... | collective-permute-start | bytes 1544 | tf_op jit(solution)/shard_map/ppermute | solution.py:170
  123.6 11.5 %collective-permute-start.5 = (f32[16,128]{1,0:T(8,128)S(1)}, f32[16,128]{1,0:T(8,128)S(1)}, u32[]{:S(2)}, u32[]{:S(2)}) collective-permute-start(f32[16,128]{1,0:T(8,128)S(1)} %broadcast_select_fusion), channel_id=1, source_target_pairs={{0,8},{8,0},{1,9},{9,1},{2,10},{10,2},{3,11},{11,3},{4,12},{12,4},... | collective-permute-start | bytes 24584 | tf_op jit(solution)/shard_map/ppermute | solution.py:170
  135.2 5.5 %collective-permute-start.6 = (f32[16,128]{1,0:T(8,128)S(1)}, f32[16,128]{1,0:T(8,128)S(1)}, u32[]{:S(2)}, u32[]{:S(2)}) collective-permute-start(f32[16,128]{1,0:T(8,128)S(1)} %fusion), channel_id=1, source_target_pairs={{0,1},{1,0},{2,3},{3,2},{4,5},{5,4},{6,7},{7,6},{8,9},{9,8},{10,11... | collective-permute-start | bytes 24584 | tf_op jit(solution)/shard_map/ppermute | solution.py:170
  140.8 6.4 %collective-permute-start.7 = (f32[16,128]{1,0:T(8,128)S(1)}, f32[16,128]{1,0:T(8,128)S(1)}, u32[]{:S(2)}, u32[]{:S(2)}) collective-permute-start(f32[16,128]{1,0:T(8,128)S(1)} %fusion.1), channel_id=1, source_target_pairs={{0,2},{1,3},{2,0},{3,1},{4,6},{5,7},{6,4},{7,5},{8,10},{9,11},{10,... | collective-permute-start | bytes 24584 | tf_op jit(solution)/shard_map/ppermute | solution.py:170
  147.3 9.4 %collective-permute-start.8 = (f32[16,128]{1,0:T(8,128)S(1)}, f32[16,128]{1,0:T(8,128)S(1)}, u32[]{:S(2)}, u32[]{:S(2)}) collective-permute-start(f32[16,128]{1,0:T(8,128)S(1)} %add.42), channel_id=1, source_target_pairs={{0,4},{1,5},{2,6},{3,7},{4,0},{5,1},{6,2},{7,3},{8,12},{9,13},{10,... | collective-permute-start | bytes 24584 | tf_op jit(solution)/shard_map/ppermute | solution.py:170

commit v2 on v1

v2 whole, which is shorter than its diff:
```python
import functools
import math

import jax
import jax.numpy as jnp
from jax import lax
from jax.experimental import pallas as pl
from jax.experimental.pallas import tpu as pltpu
from jax.sharding import Mesh, PartitionSpec as P

f32 = jnp.float32
bf16 = jnp.bfloat16
NEG = -1e30
BLOCK_Q = 512
ALONG_ROWS = (((1,), (1,)), ((), ()))
PLAIN = (((1,), (0,)), ((), ()))
VMEM = pl.BlockSpec(memory_space=pltpu.VMEM)
HBM = pl.BlockSpec(memory_space=pltpu.HBM)
SMEM = pl.BlockSpec(memory_space=pltpu.SMEM)


def dot(a, b, dims=PLAIN):
    return lax.dot_general(a, b, dims, preferred_element_type=f32)


def split_kernel(heads, size, *refs):
    sources, out_ref, staged, arrived = refs[:4], refs[4], refs[5], refs[6]
    steps = arrived.shape[1]
    rows = staged.shape[1] // steps

    def fetch(place, step):
        here = pl.ds(step * rows, rows)
        return pltpu.make_async_copy(
            sources[place].at[here], staged.at[place, here], arrived.at[place, step]
        )

    for step in range(steps):
        for place in range(4):
            fetch(place, step).start()
    for step in range(steps):
        here = pl.ds(step * rows, rows)
        for place in range(4):
            fetch(place, step).wait()
            for head in range(heads):
                out_ref[head, place, here] = staged[place, here, head * size : (head + 1) * size]


def join_kernel(heads, size, *refs):
    source, outs, staged, sent = refs[0], refs[1:5], refs[5], refs[6]
    steps = sent.shape[1]
    rows = staged.shape[1] // steps

    def store(place, step):
        here = pl.ds(step * rows, rows)
        return pltpu.make_async_copy(
            staged.at[place, here], outs[place].at[here], sent.at[place, step]
        )

    for step in range(steps):
        here = pl.ds(step * rows, rows)
        for place in range(4):
            for head in range(heads):
                staged[place, here, head * size : (head + 1) * size] = source[head, place, here]
            store(place, step).start()
    for step in range(steps):
        for place in range(4):
            store(place, step).wait()


def attention_kernel(block_q, length_ref, scale_ref, x_ref, out_ref, term_ref, *scratch):
    tokens = x_ref.shape[0] * x_ref.shape[2]
    length = length_ref[0]
    half = tokens // 2

    @pl.when(length <= half)
    def _():
        attend_keys(half, block_q, length, scale_ref, x_ref, out_ref, term_ref, *scratch)

    @pl.when(length > half)
    def _():
        attend_keys(tokens, block_q, length, scale_ref, x_ref, out_ref, term_ref, *scratch)


def attend_keys(
    width, block_q, length, scale_ref, x_ref, out_ref, term_ref,
    keys_t, values_t, scaled_ref, grads_ref, scores, expos, dprobs, dkeys, dvalues, sent_q, sent_k, results,
):
    blocks, operands, part, size = x_ref.shape
    tokens = blocks * part
    inverse = 1.0 / math.sqrt(size)
    factor = inverse * math.log2(math.e)
    q_blocks = (length + block_q - 1) // block_q
    q_parts, k_parts = block_q // part, width // part
    scale = scale_ref[...]
    rows = pl.ds(0, width)

    def rows_of(block, parts, operand):
        return x_ref[pl.ds(block * parts, parts), operand].reshape(parts * part, size)

    def query_rows(block):
        return pl.ds(pl.multiple_of(block * block_q, block_q), block_q)

    def fold(wide, op):
        return op(op(wide.reshape(width // 8, 8, block_q), axis=0), axis=0, keepdims=True)

    def valid_rows(block):
        return lax.broadcasted_iota(jnp.int32, (block_q, size), 0) + block * block_q < length

    def send_queries(block):
        here = pl.ds(block * q_parts, q_parts)
        return pltpu.make_async_copy(
            results.at[here, 0:2], out_ref.at[here, 0:2], sent_q.at[block]
        )

    def send_keys(block):
        here = pl.ds(block * q_parts, q_parts)
        return pltpu.make_async_copy(
            results.at[here, 2:4], out_ref.at[here, 2:4], sent_k.at[block]
        )

    def prepare_queries(block, carry):
        here = query_rows(block)
        scaled_ref[here, :] = (rows_of(block, q_parts, 0).astype(f32) * scale).astype(bf16)
        grads = rows_of(block, q_parts, 3).astype(f32)
        grads_ref[here, :] = jnp.where(valid_rows(block), grads, 0.0).astype(bf16)
        return carry

    def sweep(third=None, second=None, first=None):
        results_of = ()
        if third:
            block_c, share, delta = third
            scaled_c, grads_c = scaled_ref[query_rows(block_c), :], grads_ref[query_rows(block_c), :]
            probs = expos[rows, :] * share
            probs_b = probs.astype(bf16)
            dscore = (probs * (dprobs[rows, :] - delta)).astype(bf16)
            dvalues[rows, :] += dot(probs_b, grads_c)
            dkeys[rows, :] += dot(dscore, scaled_c)
            results_of += (dot(values_t[:, rows], probs_b), dot(keys_t[:, rows], dscore))
        if second:
            block_b, top = second
            dprob = dot(rows_of(0, k_parts, 2), grads_ref[query_rows(block_b), :], ALONG_ROWS)
            expo = jnp.exp2((scores[rows, :] - top) * factor)
            expos[rows, :] = expo
            dprobs[rows, :] = dprob
            share = 1.0 / fold(expo, jnp.sum)
            results_of += (share, fold(expo * dprob, jnp.sum) * share)
        if first is not None:
            raw = dot(rows_of(0, k_parts, 1), scaled_ref[query_rows(first), :], ALONG_ROWS)
            places = lax.broadcasted_iota(jnp.int32, (width, block_q), 0)
            raw = jnp.where(places < length, raw, NEG)
            scores[rows, :] = raw
            results_of += (fold(raw, jnp.max),)
        return results_of

    def finish_block(block, out_t, dscaled_t):
        attended = jnp.where(valid_rows(block), out_t.T, 0.0).astype(bf16)
        dscaled = (dscaled_t.T * inverse).astype(bf16).astype(f32)
        queries = rows_of(block, q_parts, 0).astype(f32)
        term_ref[...] += jnp.sum((dscaled * queries).reshape(block_q // 8, 8, size), axis=0)
        here = pl.ds(block * q_parts, q_parts)
        results[here, 0] = attended.reshape(q_parts, part, size)
        results[here, 1] = (dscaled * scale).astype(bf16).reshape(q_parts, part, size)
        send_queries(block).start()

    lax.fori_loop(0, q_blocks, prepare_queries, 0)
    last = q_blocks - 1
    (top,) = sweep(first=0)
    for start in range(0, width, 512):
        span = min(512, width - start)
        here = pl.ds(start, span)
        keys_t[:, here] = rows_of(start // span, span // part, 1).T
        values_t[:, here] = rows_of(start // span, span // part, 2).T
    term_ref[...] = jnp.zeros_like(term_ref)
    dkeys[rows, :] = jnp.zeros((width, size), f32)
    dvalues[rows, :] = jnp.zeros((width, size), f32)
    share, delta, top = sweep(second=(0, top), first=jnp.minimum(1, last))

    def query_block(block, carry):
        share, delta, top = carry
        after = jnp.minimum(block + 1, last)
        out_t, dscaled_t, *carry = sweep((block, share, delta), (after, top), jnp.minimum(block + 2, last))
        finish_block(block, out_t, dscaled_t)
        return tuple(carry)

    share, delta, top = lax.fori_loop(0, last, query_block, (share, delta, top))
    finish_block(last, *sweep((last, share, delta)))

    def clear_queries(block, carry):
        results[pl.ds(block * q_parts, q_parts), 0:2] = jnp.zeros((q_parts, 2, part, size), bf16)
        send_queries(block).start()
        return carry

    lax.fori_loop(q_blocks, tokens // block_q, clear_queries, 0)
    for block in range(tokens // block_q):
        here, mine = pl.ds(block * q_parts, q_parts), pl.ds(block * block_q, block_q)
        if block * block_q < width:
            results[here, 2] = (dkeys[mine, :] * inverse).astype(bf16).reshape(q_parts, part, size)
            results[here, 3] = dvalues[mine, :].astype(bf16).reshape(q_parts, part, size)
        else:
            results[here, 2:4] = jnp.zeros((q_parts, 2, part, size), bf16)
        send_keys(block).start()
    for block in range(tokens // block_q):
        send_queries(block).wait()
        send_keys(block).wait()


def attend(length, scale, x):
    blocks, _, part, size = x.shape
    tokens = blocks * part
    block_q = min(BLOCK_Q, tokens)
    copies = tokens // block_q
    return pl.pallas_call(
        functools.partial(attention_kernel, block_q),
        out_shape=(jax.ShapeDtypeStruct(x.shape, bf16), jax.ShapeDtypeStruct((8, size), f32)),
        in_specs=[SMEM, VMEM, VMEM],
        out_specs=(HBM, VMEM),
        scratch_shapes=[pltpu.VMEM((size, tokens), bf16)] * 2
        + [pltpu.VMEM((tokens, size), bf16)] * 2
        + [pltpu.VMEM((tokens, block_q), f32)] * 3
        + [pltpu.VMEM((tokens, size), f32)] * 2
        + [pltpu.SemaphoreType.DMA((copies,))] * 2
        + [pltpu.VMEM(x.shape, bf16)],
        cost_estimate=pl.CostEstimate(
            flops=12 * tokens * tokens * size, bytes_accessed=4 * x.size, transcendentals=tokens * tokens
        ),
        compiler_params=pltpu.CompilerParams(vmem_limit_bytes=48 * 1024 * 1024),
        name="attention",
    )(length, scale, x)


def per_device(queries, keys, values, grads_out, q_scale, lengths):
    heads, size = q_scale.shape
    local, width = queries.shape[1:]
    seq = ("xh", "y")
    me = lax.axis_index(seq)
    small = pltpu.CompilerParams(vmem_limit_bytes=16 * 1024 * 1024)
    steps = max(local // 32, 1)
    x = pl.pallas_call(
        functools.partial(split_kernel, heads, size),
        out_shape=jax.ShapeDtypeStruct((heads, 4, local, size), bf16),
        in_specs=[HBM] * 4,
        out_specs=VMEM,
        scratch_shapes=[
            pltpu.VMEM((4, local, width), bf16),
            pltpu.SemaphoreType.DMA((4, steps)),
        ],
        compiler_params=pltpu.CompilerParams(vmem_limit_bytes=56 * 1024 * 1024),
        name="split",
    )(queries[0], keys[0], values[0], grads_out[0])
    x = lax.all_to_all(x, seq, 0, 0, tiled=True)
    scale = lax.dynamic_slice_in_dim(q_scale, me, 1, 0)
    results, term = attend(lengths, scale, x)
    back = lax.all_to_all(results, seq, 0, 0, tiled=True)

    term = jnp.sum(term, axis=0, keepdims=True)
    across = lax.ppermute(term, "xh", [(0, 1), (1, 0)])
    own = lax.broadcasted_iota(jnp.int32, (2, size), 0) == lax.axis_index("xh")
    pair = jnp.where(own, term, across)
    for axis in ("c", "xl", "z"):
        pair = lax.psum(pair, axis)
    grid = lax.all_gather(pair, "y", axis=1).reshape(heads, size)

    outs = pl.pallas_call(
        functools.partial(join_kernel, heads, size),
        out_shape=[jax.ShapeDtypeStruct((local, width), bf16)] * 4,
        in_specs=[VMEM],
        out_specs=[HBM] * 4,
        scratch_shapes=[
            pltpu.VMEM((4, local, width), bf16),
            pltpu.SemaphoreType.DMA((4, steps)),
        ],
        compiler_params=small,
        name="join",
    )(back)
    return tuple(out[None] for out in outs) + (grid,)


def solution(mesh):
    fine = Mesh(mesh.devices.reshape(2, 8, 2, 2, 8), ("xl", "z", "c", "xh", "y"))
    tokens = P(("xl", "z", "c"), ("xh", "y"), None)
    return jax.shard_map(
        per_device,
        mesh=fine,
        in_specs=(tokens, tokens, tokens, tokens, P(), P(("xl", "z", "c"))),
        out_specs=(tokens, tokens, tokens, tokens, P()),
        check_vma=False,
    )
```

time: 160 us -> 145 us (0.906)
  the two profiles are of different devices: /device:TPU:104 before, /device:TPU:384 now
where the time goes in v2:
time: 145 us
  waiting for transfers between devices  52.2 us (36%)
  blocking collectives  49.7 us (34%)
  starting transfers between devices  20.7 us (14%)
  Pallas kernels  18.6 us (13%)
  local copies, waits for them, and re-layouts  1.96 us (1%)
    all_to_all x1, waiting for transfers between devices, per_device(): x = lax.all_to_all(x, seq, 0, 0, tiled=True)  49.8 us
    all_gather x1, blocking collectives, per_device(): grid = lax.all_gather(pair, 'y', axis=1).reshape(heads, size)  28 us
    psum x3, blocking collectives, per_device(): pair = lax.psum(pair, axis)  21.8 us
    pallas_call x1, Pallas kernels, attend(): pl.pallas_call(functools.partial(attention_kernel, block_q), out_shape=(j...  14 us
    all_to_all x1, starting transfers between devices, per_device(): x = lax.all_to_all(x, seq, 0, 0, tiled=True)  9.68 us
    all_to_all x1, starting transfers between devices, per_device(): back = lax.all_to_all(results, seq, 0, 0, tiled=True)  5.67 us
    ppermute x1, starting transfers between devices, per_device(): across = lax.ppermute(term, 'xh', [(0, 1), (1, 0)])  5.33 us
    pallas_call x1, Pallas kernels, per_device(): pl.pallas_call(functools.partial(split_kernel, heads, size), out_shape=ja...  3.11 us
  transfers between devices with their start and end apart: 3, of which 2 were waited for; matrix products, arithmetic and copies ran while one was open for 0% of the time, Pallas kernels for 0%

profile of v2, /device:TPU:384, one launch (start us, length us, event | category | flops | bytes accessed | tf_op | source)
XLA Modules:
  0.0 144.6 jit_solution(14184950397136538421)
XLA Ops:
  0.6 0.0 copy-start
  0.6 3.1 %split.1 = bf16[16,4,128,128]{3,2,1,0:T(8,128)(2,1)} custom-call(bf16[128,2048]{1,0:T(8,128)(2,1)} %bitcast.14, bf16[128,2048]{1,0:T(8,128)(2,1)} %bitcast.15, bf16[128,2048]{1,0:T(8,128)(2,1)} %bitcast.16, bf16[128,2048]{1,0:T(8,128)(2,1)} %bitcast.17), custom_call_target="tpu_custom_call" | custom-call | tf_op jit(solution)/shard_map/split/pallas_call | solution.py:238
  3.8 9.7 %all-to-all-start = ((bf16[16,4,128,128]{3,2,1,0:T(8,128)(2,1)}), bf16[16,4,128,128]{3,2,1,0:T(8,128)(2,1)S(1)}, u32[]{:S(2)}, u32[]{:S(2)}) async-start(bf16[16,4,128,128]{3,2,1,0:T(8,128)(2,1)} %split.1), calls=%async_computation | async-start | bytes 4194304 | tf_op jit(solution)/shard_map/all_to_all | solution.py:250
  14.1 0.0 copy-done
  14.1 49.8 %all-to-all-done.x_ref = bf16[16,4,128,128]{3,2,1,0:T(8,128)(2,1)S(1)} async-done(((bf16[16,4,128,128]{3,2,1,0:T(8,128)(2,1)}), bf16[16,4,128,128]{3,2,1,0:T(8,128)(2,1)S(1)}, u32[]{:S(2)}, u32[]{:S(2)}) %all-to-all-start) | async-done | bytes 2097184 | tf_op jit(solution)/shard_map/all_to_all | solution.py:250
  63.9 14.0 %attention.1 = (bf16[16,4,128,128]{3,2,1,0:T(8,128)(2,1)S(1)}, f32[8,128]{1,0:T(8,128)S(1)}) custom-call(s32[1]{0:T(128)S(6)} %copy.14.length_ref, f32[1,128]{1,0:T(1,128)S(1)} %constant_dynamic-slice_fusion.scale_ref, bf16[16,4,128,128]{3,2,1,0:T(8,128)(2,1)S(1)} %all-to-all-done.x_ref), custom_call_target="tpu_custom_call" | custom-call | flops 6442450944 | bytes 4194304 | tf_op jit(solution)/shard_map/attention/pallas_call | solution.py:212
  78.0 0.0 copy-start.1
  78.0 1.3 copy-done.1
  79.3 5.7 %all-to-all-start.1 = ((bf16[16,4,128,128]{3,2,1,0:T(8,128)(2,1)}), bf16[16,4,128,128]{3,2,1,0:T(8,128)(2,1)S(1)}, u32[]{:S(2)}, u32[]{:S(2)}) async-start(bf16[16,4,128,128]{3,2,1,0:T(8,128)(2,1)} %copy-done.1), calls=%async_computation.1 | async-start | bytes 4194304 | tf_op jit(solution)/shard_map/all_to_all | solution.py:253
  85.0 5.3 %collective-permute-start = (f32[1,128]{1,0:T(1,128)S(1)}, f32[1,128]{1,0:T(1,128)S(1)}, u32[]{:S(2)}, u32[]{:S(2)}) collective-permute-start(f32[1,128]{1,0:T(1,128)S(1)} %bitcast.20), channel_id=1, source_target_pairs={{0,8},{8,0},{1,9},{9,1},{2,10},{10,2},{3,11},{11,3},{4,12},{12,4},... | collective-permute-start | bytes 1544 | tf_op jit(solution)/shard_map/ppermute | solution.py:256
  90.4 2.4 %collective-permute-done = f32[1,128]{1,0:T(1,128)S(1)} collective-permute-done((f32[1,128]{1,0:T(1,128)S(1)}, f32[1,128]{1,0:T(1,128)S(1)}, u32[]{:S(2)}, u32[]{:S(2)}) %collective-permute-start) | collective-permute-done | bytes 544 | tf_op jit(solution)/shard_map/ppermute | solution.py:256
  92.7 0.1 broadcast_select_fusion
  92.8 2.4 %psum.21 = f32[2,128]{1,0:T(2,128)S(1)} all-reduce(f32[2,128]{1,0:T(2,128)S(1)} %broadcast_select_fusion), channel_id=1, replica_groups=mesh['xl'=2,'z'=8,'c'=2,'xh'=2,'y'=8] {'c'}, use_global_device_ids=true, to_apply=%region_1.2 | all-reduce | flops 256 | bytes 2048 | tf_op jit(solution)/shard_map/psum | solution.py:260
  95.3 4.9 %psum.22 = f32[2,128]{1,0:T(2,128)S(1)} all-reduce(f32[2,128]{1,0:T(2,128)S(1)} %psum.21), channel_id=1, replica_groups=mesh['xl'=2,'z'=8,'c'=2,'xh'=2,'y'=8] {'xl'}, use_global_device_ids=true, to_apply=%region_2.3 | all-reduce | flops 256 | bytes 2048 | tf_op jit(solution)/shard_map/psum | solution.py:260
  100.2 14.4 %psum.23 = f32[2,1,128]{2,0,1:T(2,128)S(1)} all-reduce(f32[2,1,128]{2,0,1:T(2,128)S(1)} %bitcast.19), channel_id=1, replica_groups=mesh['xl'=2,'z'=8,'c'=2,'xh'=2,'y'=8] {'z'}, use_global_device_ids=true, to_apply=%region_3.4 | all-reduce | flops 256 | bytes 2048 | tf_op jit(solution)/shard_map/psum | solution.py:260
  114.6 28.0 %all_gather.7 = f32[2,8,128]{2,0,1:T(2,128)S(1)} all-gather(f32[2,1,128]{2,0,1:T(2,128)S(1)} %psum.23), channel_id=1, replica_groups=mesh['xl'=2,'z'=8,'c'=2,'xh'=2,'y'=8] {'y'}, dimensions={1}, use_global_device_ids=true | all-gather | bytes 9216 | tf_op jit(solution)/shard_map/all_gather | solution.py:261
  142.6 0.6 copy.13
  143.2 0.0 all-to-all-done.1.refs_0_
  143.2 1.5 %join.1 = (bf16[128,2048]{1,0:T(8,128)(2,1)}, bf16[128,2048]{1,0:T(8,128)(2,1)}, bf16[128,2048]{1,0:T(8,128)(2,1)}, bf16[128,2048]{1,0:T(8,128)(2,1)}) custom-call(bf16[16,4,128,128]{3,2,1,0:T(8,128)(2,1)S(1)} %all-to-all-done.1.refs_0_), custom_call_target="tpu_custom_call" | custom-call | tf_op jit(solution)/shard_map/join/pallas_call | solution.py:263
  (3 shorter events, 0.0 us)
Async XLA Ops:
  0.6 13.5 %copy-start = (f32[16,128]{1,0:T(8,128)S(1)}, f32[16,128]{1,0:T(8,128)}, u32[]{:S(2)}) copy-start(f32[16,128]{1,0:T(8,128)} %param.10) | copy-start | bytes 24580
  3.8 60.2 %all-to-all-start = ((bf16[16,4,128,128]{3,2,1,0:T(8,128)(2,1)}), bf16[16,4,128,128]{3,2,1,0:T(8,128)(2,1)S(1)}, u32[]{:S(2)}, u32[]{:S(2)}) async-start(bf16[16,4,128,128]{3,2,1,0:T(8,128)(2,1)} %split.1), calls=%async_computation | async-start | bytes 4194304 | tf_op jit(solution)/shard_map/all_to_all | solution.py:250
  78.0 1.4 copy-start.1
  79.3 63.8 %all-to-all-start.1 = ((bf16[16,4,128,128]{3,2,1,0:T(8,128)(2,1)}), bf16[16,4,128,128]{3,2,1,0:T(8,128)(2,1)S(1)}, u32[]{:S(2)}, u32[]{:S(2)}) async-start(bf16[16,4,128,128]{3,2,1,0:T(8,128)(2,1)} %copy-done.1), calls=%async_computation.1 | async-start | bytes 4194304 | tf_op jit(solution)/shard_map/all_to_all | solution.py:253
  85.0 7.7 %collective-permute-start = (f32[1,128]{1,0:T(1,128)S(1)}, f32[1,128]{1,0:T(1,128)S(1)}, u32[]{:S(2)}, u32[]{:S(2)}) collective-permute-start(f32[1,128]{1,0:T(1,128)S(1)} %bitcast.20), channel_id=1, source_target_pairs={{0,8},{8,0},{1,9},{9,1},{2,10},{10,2},{3,11},{11,3},{4,12},{12,4},... | collective-permute-start | bytes 1544 | tf_op jit(solution)/shard_map/ppermute | solution.py:256

commit v3 on v2

--- a/solution.py
+++ b/solution.py
@@ -24,7 +24,7 @@
 
 
 def split_kernel(heads, size, *refs):
-    sources, out_ref, staged, arrived = refs[:4], refs[4], refs[5], refs[6]
+    sources, out_ref, staged, parted, arrived, sent = refs[:4], *refs[4:]
     steps = arrived.shape[1]
     rows = staged.shape[1] // steps
 
@@ -34,6 +34,12 @@
             sources[place].at[here], staged.at[place, here], arrived.at[place, step]
         )
 
+    def store(place, step):
+        here = pl.ds(step * rows, rows)
+        return pltpu.make_async_copy(
+            parted.at[:, place, here], out_ref.at[:, place, here], sent.at[place, step]
+        )
+
     for step in range(steps):
         for place in range(4):
             fetch(place, step).start()
@@ -42,7 +48,11 @@
         for place in range(4):
             fetch(place, step).wait()
             for head in range(heads):
-                out_ref[head, place, here] = staged[place, here, head * size : (head + 1) * size]
+                parted[head, place, here] = staged[place, here, head * size : (head + 1) * size]
+            store(place, step).start()
+    for step in range(steps):
+        for place in range(4):
+            store(place, step).wait()
 
 
 def join_kernel(heads, size, *refs):
@@ -239,9 +249,11 @@
         functools.partial(split_kernel, heads, size),
         out_shape=jax.ShapeDtypeStruct((heads, 4, local, size), bf16),
         in_specs=[HBM] * 4,
-        out_specs=VMEM,
+        out_specs=HBM,
         scratch_shapes=[
             pltpu.VMEM((4, local, width), bf16),
+            pltpu.VMEM((heads, 4, local, size), bf16),
+            pltpu.SemaphoreType.DMA((4, steps)),
             pltpu.SemaphoreType.DMA((4, steps)),
         ],
         compiler_params=pltpu.CompilerParams(vmem_limit_bytes=56 * 1024 * 1024),

time: 145 us -> 144 us (level)
  the two profiles are of different devices: /device:TPU:384 before, /device:TPU:326 now
where the time goes in v3:
time: 144 us
  waiting for transfers between devices  52.7 us (37%)
  blocking collectives  50 us (35%)
  starting transfers between devices  19.8 us (14%)
  Pallas kernels  18.1 us (13%)
  local copies, waits for them, and re-layouts  1.96 us (1%)
    all_to_all x1, waiting for transfers between devices, per_device(): x = lax.all_to_all(x, seq, 0, 0, tiled=True)  47.7 us
    all_gather x1, blocking collectives, per_device(): grid = lax.all_gather(pair, 'y', axis=1).reshape(heads, size)  29 us
    psum x3, blocking collectives, per_device(): pair = lax.psum(pair, axis)  21 us
    pallas_call x1, Pallas kernels, attend(): pl.pallas_call(functools.partial(attention_kernel, block_q), out_shape=(j...  14 us
    all_to_all x1, starting transfers between devices, per_device(): x = lax.all_to_all(x, seq, 0, 0, tiled=True)  10.1 us
    all_to_all x1, starting transfers between devices, per_device(): back = lax.all_to_all(results, seq, 0, 0, tiled=True)  7.72 us
    ppermute x1, waiting for transfers between devices, per_device(): across = lax.ppermute(term, 'xh', [(0, 1), (1, 0)])  4.96 us
  transfers between devices with their start and end apart: 3, of which 2 were waited for; matrix products, arithmetic and copies ran while one was open for 0% of the time, Pallas kernels for 0%

profile of v3, /device:TPU:326, one launch (start us, length us, event | category | flops | bytes accessed | tf_op | source)
XLA Modules:
  0.0 144.1 jit_solution(16773865196043084463)
XLA Ops:
  0.6 0.0 copy-start
  0.6 2.6 %split.1 = bf16[16,4,128,128]{3,2,1,0:T(8,128)(2,1)} custom-call(bf16[128,2048]{1,0:T(8,128)(2,1)} %bitcast.14, bf16[128,2048]{1,0:T(8,128)(2,1)} %bitcast.15, bf16[128,2048]{1,0:T(8,128)(2,1)} %bitcast.16, bf16[128,2048]{1,0:T(8,128)(2,1)} %bitcast.17), custom_call_target="tpu_custom_call" | custom-call | tf_op jit(solution)/shard_map/split/pallas_call | solution.py:248
  3.3 10.1 %all-to-all-start = ((bf16[16,4,128,128]{3,2,1,0:T(8,128)(2,1)}), bf16[16,4,128,128]{3,2,1,0:T(8,128)(2,1)S(1)}, u32[]{:S(2)}, u32[]{:S(2)}) async-start(bf16[16,4,128,128]{3,2,1,0:T(8,128)(2,1)} %split.1), calls=%async_computation | async-start | bytes 4194304 | tf_op jit(solution)/shard_map/all_to_all | solution.py:262
  14.0 0.0 copy-done
  14.1 47.7 %all-to-all-done.x_ref = bf16[16,4,128,128]{3,2,1,0:T(8,128)(2,1)S(1)} async-done(((bf16[16,4,128,128]{3,2,1,0:T(8,128)(2,1)}), bf16[16,4,128,128]{3,2,1,0:T(8,128)(2,1)S(1)}, u32[]{:S(2)}, u32[]{:S(2)}) %all-to-all-start) | async-done | bytes 2097184 | tf_op jit(solution)/shard_map/all_to_all | solution.py:262
  61.8 14.0 %attention.1 = (bf16[16,4,128,128]{3,2,1,0:T(8,128)(2,1)S(1)}, f32[8,128]{1,0:T(8,128)S(1)}) custom-call(s32[1]{0:T(128)S(6)} %copy.14.length_ref, f32[1,128]{1,0:T(1,128)S(1)} %constant_dynamic-slice_fusion.scale_ref, bf16[16,4,128,128]{3,2,1,0:T(8,128)(2,1)S(1)} %all-to-all-done.x_ref), custom_call_target="tpu_custom_call" | custom-call | flops 6442450944 | bytes 4194304 | tf_op jit(solution)/shard_map/attention/pallas_call | solution.py:222
  75.8 0.0 copy-start.1
  75.9 1.3 copy-done.1
  77.2 7.7 %all-to-all-start.1 = ((bf16[16,4,128,128]{3,2,1,0:T(8,128)(2,1)}), bf16[16,4,128,128]{3,2,1,0:T(8,128)(2,1)S(1)}, u32[]{:S(2)}, u32[]{:S(2)}) async-start(bf16[16,4,128,128]{3,2,1,0:T(8,128)(2,1)} %copy-done.1), calls=%async_computation.1 | async-start | bytes 4194304 | tf_op jit(solution)/shard_map/all_to_all | solution.py:265
  84.9 2.0 %collective-permute-start = (f32[1,128]{1,0:T(1,128)S(1)}, f32[1,128]{1,0:T(1,128)S(1)}, u32[]{:S(2)}, u32[]{:S(2)}) collective-permute-start(f32[1,128]{1,0:T(1,128)S(1)} %bitcast.20), channel_id=1, source_target_pairs={{0,8},{8,0},{1,9},{9,1},{2,10},{10,2},{3,11},{11,3},{4,12},{12,4},... | collective-permute-start | bytes 1544 | tf_op jit(solution)/shard_map/ppermute | solution.py:268
  87.0 5.0 %collective-permute-done = f32[1,128]{1,0:T(1,128)S(1)} collective-permute-done((f32[1,128]{1,0:T(1,128)S(1)}, f32[1,128]{1,0:T(1,128)S(1)}, u32[]{:S(2)}, u32[]{:S(2)}) %collective-permute-start) | collective-permute-done | bytes 544 | tf_op jit(solution)/shard_map/ppermute | solution.py:268
  91.9 0.1 broadcast_select_fusion
  92.0 2.4 %psum.21 = f32[2,128]{1,0:T(2,128)S(1)} all-reduce(f32[2,128]{1,0:T(2,128)S(1)} %broadcast_select_fusion), channel_id=1, replica_groups=mesh['xl'=2,'z'=8,'c'=2,'xh'=2,'y'=8] {'c'}, use_global_device_ids=true, to_apply=%region_1.2 | all-reduce | flops 256 | bytes 2048 | tf_op jit(solution)/shard_map/psum | solution.py:272
  94.4 5.1 %psum.22 = f32[2,128]{1,0:T(2,128)S(1)} all-reduce(f32[2,128]{1,0:T(2,128)S(1)} %psum.21), channel_id=1, replica_groups=mesh['xl'=2,'z'=8,'c'=2,'xh'=2,'y'=8] {'xl'}, use_global_device_ids=true, to_apply=%region_2.3 | all-reduce | flops 256 | bytes 2048 | tf_op jit(solution)/shard_map/psum | solution.py:272
  99.5 13.5 %psum.23 = f32[2,1,128]{2,0,1:T(2,128)S(1)} all-reduce(f32[2,1,128]{2,0,1:T(2,128)S(1)} %bitcast.19), channel_id=1, replica_groups=mesh['xl'=2,'z'=8,'c'=2,'xh'=2,'y'=8] {'z'}, use_global_device_ids=true, to_apply=%region_3.4 | all-reduce | flops 256 | bytes 2048 | tf_op jit(solution)/shard_map/psum | solution.py:272
  113.0 29.0 %all_gather.7 = f32[2,8,128]{2,0,1:T(2,128)S(1)} all-gather(f32[2,1,128]{2,0,1:T(2,128)S(1)} %psum.23), channel_id=1, replica_groups=mesh['xl'=2,'z'=8,'c'=2,'xh'=2,'y'=8] {'y'}, dimensions={1}, use_global_device_ids=true | all-gather | bytes 9216 | tf_op jit(solution)/shard_map/all_gather | solution.py:273
  142.0 0.6 copy.13
  142.6 0.0 all-to-all-done.1.refs_0_
  142.6 1.5 %join.1 = (bf16[128,2048]{1,0:T(8,128)(2,1)}, bf16[128,2048]{1,0:T(8,128)(2,1)}, bf16[128,2048]{1,0:T(8,128)(2,1)}, bf16[128,2048]{1,0:T(8,128)(2,1)}) custom-call(bf16[16,4,128,128]{3,2,1,0:T(8,128)(2,1)S(1)} %all-to-all-done.1.refs_0_), custom_call_target="tpu_custom_call" | custom-call | tf_op jit(solution)/shard_map/join/pallas_call | solution.py:275
  (3 shorter events, 0.0 us)
Async XLA Ops:
  0.6 13.4 %copy-start = (f32[16,128]{1,0:T(8,128)S(1)}, f32[16,128]{1,0:T(8,128)}, u32[]{:S(2)}) copy-start(f32[16,128]{1,0:T(8,128)} %param.10) | copy-start | bytes 24580
  3.3 58.5 %all-to-all-start = ((bf16[16,4,128,128]{3,2,1,0:T(8,128)(2,1)}), bf16[16,4,128,128]{3,2,1,0:T(8,128)(2,1)S(1)}, u32[]{:S(2)}, u32[]{:S(2)}) async-start(bf16[16,4,128,128]{3,2,1,0:T(8,128)(2,1)} %split.1), calls=%async_computation | async-start | bytes 4194304 | tf_op jit(solution)/shard_map/all_to_all | solution.py:262
  75.8 1.4 copy-start.1
  77.2 65.4 %all-to-all-start.1 = ((bf16[16,4,128,128]{3,2,1,0:T(8,128)(2,1)}), bf16[16,4,128,128]{3,2,1,0:T(8,128)(2,1)S(1)}, u32[]{:S(2)}, u32[]{:S(2)}) async-start(bf16[16,4,128,128]{3,2,1,0:T(8,128)(2,1)} %copy-done.1), calls=%async_computation.1 | async-start | bytes 4194304 | tf_op jit(solution)/shard_map/all_to_all | solution.py:265
  84.9 7.0 %collective-permute-start = (f32[1,128]{1,0:T(1,128)S(1)}, f32[1,128]{1,0:T(1,128)S(1)}, u32[]{:S(2)}, u32[]{:S(2)}) collective-permute-start(f32[1,128]{1,0:T(1,128)S(1)} %bitcast.20), channel_id=1, source_target_pairs={{0,8},{8,0},{1,9},{9,1},{2,10},{10,2},{3,11},{11,3},{4,12},{12,4},... | collective-permute-start | bytes 1544 | tf_op jit(solution)/shard_map/ppermute | solution.py:268

commit v4 on v3

--- a/solution.py
+++ b/solution.py
@@ -77,7 +77,8 @@
             store(place, step).wait()
 
 
-def attention_kernel(block_q, length_ref, scale_ref, x_ref, out_ref, term_ref, *scratch):
+def attention_kernel(block_q, length_ref, scale_ref, x_ref, spent_ref, out_ref, term_ref, *scratch):
+    del spent_ref
     tokens = x_ref.shape[0] * x_ref.shape[2]
     length = length_ref[0]
     half = tokens // 2
@@ -214,7 +215,7 @@
         send_keys(block).wait()
 
 
-def attend(length, scale, x):
+def attend(length, scale, x, spent):
     blocks, _, part, size = x.shape
     tokens = blocks * part
     block_q = min(BLOCK_Q, tokens)
@@ -222,8 +223,9 @@
     return pl.pallas_call(
         functools.partial(attention_kernel, block_q),
         out_shape=(jax.ShapeDtypeStruct(x.shape, bf16), jax.ShapeDtypeStruct((8, size), f32)),
-        in_specs=[SMEM, VMEM, VMEM],
+        in_specs=[SMEM, VMEM, VMEM, HBM],
         out_specs=(HBM, VMEM),
+        input_output_aliases={3: 0},
         scratch_shapes=[pltpu.VMEM((size, tokens), bf16)] * 2
         + [pltpu.VMEM((tokens, size), bf16)] * 2
         + [pltpu.VMEM((tokens, block_q), f32)] * 3
@@ -235,7 +237,7 @@
         ),
         compiler_params=pltpu.CompilerParams(vmem_limit_bytes=48 * 1024 * 1024),
         name="attention",
-    )(length, scale, x)
+    )(length, scale, x, spent)
 
 
 def per_device(queries, keys, values, grads_out, q_scale, lengths):
@@ -259,9 +261,10 @@
         compiler_params=pltpu.CompilerParams(vmem_limit_bytes=56 * 1024 * 1024),
         name="split",
     )(queries[0], keys[0], values[0], grads_out[0])
+    spent = x
     x = lax.all_to_all(x, seq, 0, 0, tiled=True)
     scale = lax.dynamic_slice_in_dim(q_scale, me, 1, 0)
-    results, term = attend(lengths, scale, x)
+    results, term = attend(lengths, scale, x, spent)
     back = lax.all_to_all(results, seq, 0, 0, tiled=True)
 
     term = jnp.sum(term, axis=0, keepdims=True)

time: 144 us -> 144 us (level)
  the two profiles are of different devices: /device:TPU:326 before, /device:TPU:320 now
where the time goes in v4:
time: 144 us
  waiting for transfers between devices  52.2 us (36%)
  blocking collectives  49.7 us (35%)
  starting transfers between devices  20.7 us (14%)
  Pallas kernels  18.9 us (13%)
    all_to_all x1, waiting for transfers between devices, per_device(): x = lax.all_to_all(x, seq, 0, 0, tiled=True)  49.8 us
    all_gather x1, blocking collectives, per_device(): grid = lax.all_gather(pair, 'y', axis=1).reshape(heads, size)  27 us
    psum x3, blocking collectives, per_device(): pair = lax.psum(pair, axis)  22.8 us
    pallas_call x1, Pallas kernels, attend(): pl.pallas_call(functools.partial(attention_kernel, block_q), out_shape=(j...  14.8 us
    all_to_all x1, starting transfers between devices, per_device(): x = lax.all_to_all(x, seq, 0, 0, tiled=True)  9.68 us
    all_to_all x1, starting transfers between devices, per_device(): back = lax.all_to_all(results, seq, 0, 0, tiled=True)  5.68 us
    ppermute x1, starting transfers between devices, per_device(): across = lax.ppermute(term, 'xh', [(0, 1), (1, 0)])  5.33 us
  transfers between devices with their start and end apart: 3, of which 2 were waited for; matrix products, arithmetic and copies ran while one was open for 0% of the time, Pallas kernels for 0%

profile of v4, /device:TPU:320, one launch (start us, length us, event | category | flops | bytes accessed | tf_op | source)
XLA Modules:
  0.0 143.5 jit_solution(10968159699098648095)
XLA Ops:
  0.6 0.0 copy-start
  0.6 2.6 %split.1.spent_ref = bf16[16,4,128,128]{3,2,1,0:T(8,128)(2,1)} custom-call(bf16[128,2048]{1,0:T(8,128)(2,1)} %bitcast.14, bf16[128,2048]{1,0:T(8,128)(2,1)} %bitcast.15, bf16[128,2048]{1,0:T(8,128)(2,1)} %bitcast.16, bf16[128,2048]{1,0:T(8,128)(2,1)} %bitcast.17), custom_call_target="tpu_custom_call" | custom-call | tf_op jit(solution)/shard_map/split/pallas_call | solution.py:250
  3.3 9.7 %all-to-all-start = ((bf16[16,4,128,128]{3,2,1,0:T(8,128)(2,1)}), bf16[16,4,128,128]{3,2,1,0:T(8,128)(2,1)S(1)}, u32[]{:S(2)}, u32[]{:S(2)}) async-start(bf16[16,4,128,128]{3,2,1,0:T(8,128)(2,1)} %split.1.spent_ref), calls=%async_computation | async-start | bytes 4194304 | tf_op jit(solution)/shard_map/all_to_all | solution.py:265
  13.6 0.0 copy-done
  13.7 49.8 %all-to-all-done.x_ref = bf16[16,4,128,128]{3,2,1,0:T(8,128)(2,1)S(1)} async-done(((bf16[16,4,128,128]{3,2,1,0:T(8,128)(2,1)}), bf16[16,4,128,128]{3,2,1,0:T(8,128)(2,1)S(1)}, u32[]{:S(2)}, u32[]{:S(2)}) %all-to-all-start) | async-done | bytes 2097184 | tf_op jit(solution)/shard_map/all_to_all | solution.py:265
  63.5 14.8 %attention.1 = (bf16[16,4,128,128]{3,2,1,0:T(8,128)(2,1)}, f32[8,128]{1,0:T(8,128)S(1)}) custom-call(s32[1]{0:T(128)S(6)} %copy.16.length_ref, f32[1,128]{1,0:T(1,128)S(1)} %constant_dynamic-slice_fusion.scale_ref, bf16[16,4,128,128]{3,2,1,0:T(8,128)(2,1)S(1)} %all-to-all-done.x_ref, ...), custom_call_target="tpu_custom_call", output_to_operand_aliasing={{0}: (3, {})} | custom-call | flops 6442450944 | bytes 4194304 | tf_op jit(solution)/shard_map/attention/pallas_call | solution.py:223
  78.2 5.7 %all-to-all-start.1 = ((bf16[16,4,128,128]{3,2,1,0:T(8,128)(2,1)}), bf16[16,4,128,128]{3,2,1,0:T(8,128)(2,1)S(1)}, u32[]{:S(2)}, u32[]{:S(2)}) async-start(bf16[16,4,128,128]{3,2,1,0:T(8,128)(2,1)} %get-tuple-element.11), calls=%async_computation.1 | async-start | bytes 4194304 | tf_op jit(solution)/shard_map/all_to_all | solution.py:268
  83.9 5.3 %collective-permute-start = (f32[1,128]{1,0:T(1,128)S(1)}, f32[1,128]{1,0:T(1,128)S(1)}, u32[]{:S(2)}, u32[]{:S(2)}) collective-permute-start(f32[1,128]{1,0:T(1,128)S(1)} %bitcast.20), channel_id=1, source_target_pairs={{0,8},{8,0},{1,9},{9,1},{2,10},{10,2},{3,11},{11,3},{4,12},{12,4},... | collective-permute-start | bytes 1544 | tf_op jit(solution)/shard_map/ppermute | solution.py:271
  89.3 2.4 %collective-permute-done = f32[1,128]{1,0:T(1,128)S(1)} collective-permute-done((f32[1,128]{1,0:T(1,128)S(1)}, f32[1,128]{1,0:T(1,128)S(1)}, u32[]{:S(2)}, u32[]{:S(2)}) %collective-permute-start) | collective-permute-done | bytes 544 | tf_op jit(solution)/shard_map/ppermute | solution.py:271
  91.7 0.1 broadcast_select_fusion
  91.7 2.4 %psum.21 = f32[2,128]{1,0:T(2,128)S(1)} all-reduce(f32[2,128]{1,0:T(2,128)S(1)} %broadcast_select_fusion), channel_id=1, replica_groups=mesh['xl'=2,'z'=8,'c'=2,'xh'=2,'y'=8] {'c'}, use_global_device_ids=true, to_apply=%region_1.2 | all-reduce | flops 256 | bytes 2048 | tf_op jit(solution)/shard_map/psum | solution.py:275
  94.2 5.1 %psum.22 = f32[2,128]{1,0:T(2,128)S(1)} all-reduce(f32[2,128]{1,0:T(2,128)S(1)} %psum.21), channel_id=1, replica_groups=mesh['xl'=2,'z'=8,'c'=2,'xh'=2,'y'=8] {'xl'}, use_global_device_ids=true, to_apply=%region_2.3 | all-reduce | flops 256 | bytes 2048 | tf_op jit(solution)/shard_map/psum | solution.py:275
  99.2 15.3 %psum.23 = f32[2,1,128]{2,0,1:T(2,128)S(1)} all-reduce(f32[2,1,128]{2,0,1:T(2,128)S(1)} %bitcast.19), channel_id=1, replica_groups=mesh['xl'=2,'z'=8,'c'=2,'xh'=2,'y'=8] {'z'}, use_global_device_ids=true, to_apply=%region_3.4 | all-reduce | flops 256 | bytes 2048 | tf_op jit(solution)/shard_map/psum | solution.py:275
  114.5 27.0 %all_gather.7 = f32[2,8,128]{2,0,1:T(2,128)S(1)} all-gather(f32[2,1,128]{2,0,1:T(2,128)S(1)} %psum.23), channel_id=1, replica_groups=mesh['xl'=2,'z'=8,'c'=2,'xh'=2,'y'=8] {'y'}, dimensions={1}, use_global_device_ids=true | all-gather | bytes 9216 | tf_op jit(solution)/shard_map/all_gather | solution.py:276
  141.5 0.6 copy.14
  142.1 0.0 all-to-all-done.1.refs_0_
  142.1 1.5 %join.1 = (bf16[128,2048]{1,0:T(8,128)(2,1)}, bf16[128,2048]{1,0:T(8,128)(2,1)}, bf16[128,2048]{1,0:T(8,128)(2,1)}, bf16[128,2048]{1,0:T(8,128)(2,1)}) custom-call(bf16[16,4,128,128]{3,2,1,0:T(8,128)(2,1)S(1)} %all-to-all-done.1.refs_0_), custom_call_target="tpu_custom_call" | custom-call | tf_op jit(solution)/shard_map/join/pallas_call | solution.py:278
  (3 shorter events, 0.0 us)
Async XLA Ops:
  0.6 13.0 %copy-start = (f32[16,128]{1,0:T(8,128)S(1)}, f32[16,128]{1,0:T(8,128)}, u32[]{:S(2)}) copy-start(f32[16,128]{1,0:T(8,128)} %param.10) | copy-start | bytes 24580
  3.3 60.2 %all-to-all-start = ((bf16[16,4,128,128]{3,2,1,0:T(8,128)(2,1)}), bf16[16,4,128,128]{3,2,1,0:T(8,128)(2,1)S(1)}, u32[]{:S(2)}, u32[]{:S(2)}) async-start(bf16[16,4,128,128]{3,2,1,0:T(8,128)(2,1)} %split.1.spent_ref), calls=%async_computation | async-start | bytes 4194304 | tf_op jit(solution)/shard_map/all_to_all | solution.py:265
  78.2 63.9 %all-to-all-start.1 = ((bf16[16,4,128,128]{3,2,1,0:T(8,128)(2,1)}), bf16[16,4,128,128]{3,2,1,0:T(8,128)(2,1)S(1)}, u32[]{:S(2)}, u32[]{:S(2)}) async-start(bf16[16,4,128,128]{3,2,1,0:T(8,128)(2,1)} %get-tuple-element.11), calls=%async_computation.1 | async-start | bytes 4194304 | tf_op jit(solution)/shard_map/all_to_all | solution.py:268
  83.9 7.7 %collective-permute-start = (f32[1,128]{1,0:T(1,128)S(1)}, f32[1,128]{1,0:T(1,128)S(1)}, u32[]{:S(2)}, u32[]{:S(2)}) collective-permute-start(f32[1,128]{1,0:T(1,128)S(1)} %bitcast.20), channel_id=1, source_target_pairs={{0,8},{8,0},{1,9},{9,1},{2,10},{10,2},{3,11},{11,3},{4,12},{12,4},... | collective-permute-start | bytes 1544 | tf_op jit(solution)/shard_map/ppermute | solution.py:271
